TPU v7x, 512 devices: a whole 4x8x8 slice. The times are simulated.
512 devices in a mesh: seq: 64 (over x, y, core), group: 8 (over z).
Axes of the slice: x: 4, y: 8, z: 8, core: 2. Of those that a mesh axis runs over, the one named last changes fastest.
Arguments:
- queries: bfloat16 [8, 16384, 4096], P('group', 'seq'), may hold values from -4.75 to 4.75
- keys_values: bfloat16 [8, 16384, 1024], P('group', 'seq'), may hold values from -4.75 to 4.75
- block_list: int32 [8, 128, 8], P('group', 'seq'), may hold values from 0 to 127, as said below
- value_dir: bfloat16 [4096], replicated, may hold values from -2 to 2
- base_values: float32 [8, 16384], P('group', 'seq'), may hold values from -6 to 6
- rewards: float32 [8, 16384], P('group', 'seq'), may hold values from -0.4375 to 0.4375
- turn_start: int32 [8, 16384], P('group', 'seq'), may hold values 0 or 1
- actor_shard: int32 [8, 16384], P('group', 'seq'), may hold values from 0 to 511, as said below
Outputs:
- token_values: float32 [8, 16384], P('group', 'seq')
- actor_advantages: float32 [131072], P(('seq', 'group'))
- actor_returns: float32 [131072], P(('seq', 'group'))
Inputs may be any that keep to these rules, and one draw needn't show every extreme that they name: `block_list`: entry j of block b's list is a block of [max(0, b - 14), b]; an entry equal to b lists nothing. `actor_shard`: each sequence shard sends 256 // 8 of its positions to each group index of the actor's shards; of the positions held by the 8 shards of one seq index that go to one group index, exactly 4 go to each seq index. The actor's shard d has seq index d // 8 and group index d % 8.
All inputs are finite; a program needn't handle non-finite values. No bound on the sum of `turn_start` on one device may be relied on, other than what follows from the above.
Results may differ from a plain program's by a relative error of at most 0.0049.
Values may be sent and summed in bfloat16 or wider, within the bound.
No kernel may reach another device: no remote copies, remote signals or barrier semaphores. Data moves between devices by JAX's collectives and lax.ppermute only.
A program may use at most 64 MiB of HBM per device.

v0:
```python
import jax
import jax.numpy as jnp
from jax import lax
from jax.sharding import PartitionSpec as P

HD = 128
BLK = 128
WIN = 7


TRACE = 0.995


def from_behind(value, axis, steps):
    count = lax.axis_size(axis)
    initial, last = (max(0, -steps), min(count, count - steps))
    return lax.ppermute(value, axis, [(source, source + steps) for source in range(initial, last)])


def listed_mask(entries, block):
    count = entries.shape[0]
    earlier = entries < block
    same = entries[:, None] == entries[None, :]
    before = jnp.arange(count)[None, :] < jnp.arange(count)[:, None]
    repeat = jnp.any(same & before, axis=1)
    return earlier & jnp.logical_not(repeat)


def block_scores(query_block, kv_block, half, kv_heads):
    keys = kv_block[:, :half].reshape(BLK, kv_heads, HD)
    scores = jnp.einsum("qkgd,skd->kgqs", query_block, keys, preferred_element_type=jnp.float32)
    return scores * HD ** (-0.5)


def block_output(shares, kv_block, half, kv_heads):
    values = kv_block[:, half:].reshape(BLK, kv_heads, HD)
    return jnp.einsum(
        "kgqs,skd->kgqd", shares.astype(jnp.bfloat16), values, preferred_element_type=jnp.float32
    )


def attend_block(
    query_block, table, entries, block_id, local_block, shard, blocks_here, half, kv_heads
):
    valid = listed_mask(entries, block_id)
    width = entries.shape[0]
    order = jnp.argsort(jnp.where(valid, 0, 1) * width + jnp.arange(width))
    compact = entries[order]
    slots = (shard - compact // blocks_here) * blocks_here + compact % blocks_here
    count = jnp.sum(valid.astype(jnp.int32))
    own = table[local_block]
    scores = block_scores(query_block, own, half, kv_heads)
    causal = jnp.arange(BLK)[None, :] <= jnp.arange(BLK)[:, None]
    scores = jnp.where(causal, scores, -1e30)
    peak = jnp.max(scores, axis=-1)
    probs = jnp.exp(scores - peak[..., None])
    total = jnp.sum(probs, axis=-1)
    summed = block_output(probs, own, half, kv_heads)

    def visit(step, carry):
        peak, total, summed = carry
        kv_block = table[slots[step]]
        scores = block_scores(query_block, kv_block, half, kv_heads)
        new_peak = jnp.maximum(peak, jnp.max(scores, axis=-1))
        rescale = jnp.exp(peak - new_peak)
        probs = jnp.exp(scores - new_peak[..., None])
        total = total * rescale + jnp.sum(probs, axis=-1)
        summed = summed * rescale[..., None] + block_output(probs, kv_block, half, kv_heads)
        return (new_peak, total, summed)

    peak, total, summed = lax.fori_loop(0, count, visit, (peak, total, summed))
    result = summed / total[..., None]
    return jnp.transpose(result, (2, 0, 1, 3)).reshape(BLK, -1).astype(jnp.bfloat16)


def token_maps(values, gains, starts):
    eye = jnp.eye(3, dtype=jnp.float32)
    head = jnp.array([[TRACE, 1.0, 1.0], [0.0, 0.0, 0.0], [0.0, 0.0, 0.0]], jnp.float32)
    maps = jnp.where(starts[:, None, None], head[None], eye[None])
    zero = jnp.zeros_like(values)
    opening = jnp.stack([gains - values, values, zero], axis=1)
    inside = jnp.stack([zero, zero, gains], axis=1)
    offsets = jnp.where(starts[:, None], opening, inside)
    return (maps, offsets)


def compose(first, second):
    first_map, first_off = first
    second_map, second_off = second
    merged = jnp.einsum(
        "...ij,...jk->...ik", second_map, first_map, precision=lax.Precision.HIGHEST
    )
    moved = jnp.einsum("...ij,...j->...i", second_map, first_off, precision=lax.Precision.HIGHEST)
    return (merged, moved + second_off)


def bucket(data, keys, count):
    rows = data.shape[0]
    tok = keys.shape[0]
    per = tok // count
    onehot = (keys[:, None] == jnp.arange(count)[None, :]).astype(jnp.int32)
    rank = jnp.sum(onehot * (jnp.cumsum(onehot, axis=0) - 1), axis=1)
    position = keys * per + rank
    buffer = jnp.zeros((rows, tok), data.dtype).at[:, position].set(data)
    return jnp.transpose(buffer.reshape(rows, count, per), (1, 0, 2))


def shards(
    queries, keys_values, block_list, value_dir, base_values, rewards, turn_start, actor_shard
):
    tok = queries.shape[1]
    blocks_here = tok // BLK
    width = keys_values.shape[2]
    half = width // 2
    heads = queries.shape[2] // HD
    kv_heads = half // HD
    shard = lax.axis_index("seq")
    local_kv = keys_values[0]
    pieces = [local_kv]
    for distance in range(1, WIN + 1):
        pieces.append(from_behind(local_kv, "seq", distance))
    window = jnp.stack(pieces)
    table = window.reshape((WIN + 1) * blocks_here, BLK, width)
    query_rows = queries[0].reshape(blocks_here, BLK, kv_heads, heads // kv_heads, HD)
    outputs = []
    for local_block in range(blocks_here):
        block_id = shard * blocks_here + local_block
        outputs.append(
            attend_block(
                query_rows[local_block],
                table,
                block_list[0, local_block],
                block_id,
                local_block,
                shard,
                blocks_here,
                half,
                kv_heads,
            )
        )
    attended = jnp.concatenate(outputs, axis=0)
    values = jnp.dot(attended, value_dir, preferred_element_type=jnp.float32) + base_values[0]
    positions = shard * tok + jnp.arange(tok)
    starts = (turn_start[0] == 1) | (positions == 0)
    maps, offsets = token_maps(values, rewards[0], starts)
    inclusive_map, inclusive_off = lax.associative_scan(compose, (maps[::-1], offsets[::-1]))
    summary_map = inclusive_map[-1]
    summary_off = inclusive_off[-1]

    def relay_step(step, incoming):
        passed = jnp.dot(summary_map, incoming, precision=lax.Precision.HIGHEST) + summary_off
        return from_behind(passed, "seq", -1)

    incoming = lax.fori_loop(0, lax.axis_size("seq") - 1, relay_step, jnp.zeros((3,), jnp.float32))
    eye = jnp.eye(3, dtype=jnp.float32)
    before_map = jnp.concatenate([eye[None], inclusive_map[:-1]], axis=0)
    before_off = jnp.concatenate([jnp.zeros((1, 3), jnp.float32), inclusive_off[:-1]], axis=0)
    states = (
        jnp.einsum("tij,j->ti", before_map, incoming, precision=lax.Precision.HIGHEST) + before_off
    )[::-1]
    advantage = states[:, 2] + rewards[0] + states[:, 1] + TRACE * states[:, 0] - values
    returns = advantage + values
    groups_n = lax.axis_size("group")
    shards_n = lax.axis_size("seq")
    dest = actor_shard[0]
    dest_group = dest % groups_n
    dest_shard = dest // groups_n
    payload = jnp.stack([advantage, returns])
    sectioned = bucket(payload, dest_group, groups_n)
    sectioned_tags = bucket(dest_shard[None], dest_group, groups_n)
    received, tags = (
        lax.all_to_all(sectioned, "group", split_axis=0, concat_axis=0, tiled=True),
        lax.all_to_all(sectioned_tags, "group", split_axis=0, concat_axis=0, tiled=True),
    )
    middle = jnp.transpose(received, (1, 0, 2)).reshape(2, tok)
    middle_tags = tags.reshape(tok)
    second = bucket(middle, middle_tags, shards_n)
    arrived = lax.all_to_all(second, "seq", split_axis=0, concat_axis=0, tiled=True)
    final = jnp.transpose(arrived, (1, 0, 2)).reshape(2, tok)
    return (values[None], final[0], final[1])


def solution(mesh):
    placed = (
        P("group", "seq", None),
        P("group", "seq", None),
        P("group", "seq", None),
        P(),
        P("group", "seq"),
        P("group", "seq"),
        P("group", "seq"),
        P("group", "seq"),
    )
    return jax.shard_map(
        shards,
        mesh=mesh,
        in_specs=placed,
        out_specs=(P("group", "seq"), P(("seq", "group")), P(("seq", "group"))),
        check_vma=False,
    )
```

profile of v0, /device:TPU:1, one launch (start us, length us, event | category | flops | bytes accessed | tf_op | source)
XLA Modules:
  0.0 803.7 jit_solution(12497315780811636042)
XLA Ops:
  22.8 10.0 %all-to-all-start = ((s32[8,1,32]{2,1,0:T(1,128)}), s32[8,1,32]{2,1,0:T(1,128)S(1)}, u32[]{:S(2)}, u32[]{:S(2)}) async-start(s32[8,1,32]{2,1,0:T(1,128)} %transpose_reshape.3), calls=%async_computation | async-start | bytes 8192 | tf_op jit(solution)/shard_map/all_to_all | solution.py:173
  81.2 5.2 collective-permute-start.6
  96.8 6.9 collective-permute-done.5
  104.6 32.2 %collective-permute-done.6 = bf16[256,1024]{1,0:T(8,128)(2,1)S(1)} collective-permute-done((bf16[256,1024]{1,0:T(8,128)(2,1)}, bf16[256,1024]{1,0:T(8,128)(2,1)S(1)}, u32[]{:S(2)}, u32[]{:S(2)}) %collective-permute-start.6) | collective-permute-done | bytes 524320 | tf_op jit(solution)/shard_map/ppermute | solution.py:17
  137.6 28.7 %collective-permute-done.7 = bf16[256,1024]{1,0:T(8,128)(2,1)S(1)} collective-permute-done((bf16[256,1024]{1,0:T(8,128)(2,1)S(1)}, bf16[256,1024]{1,0:T(8,128)(2,1)S(1)}, u32[]{:S(2)}, u32[]{:S(2)}) %collective-permute-start.7) | collective-permute-done | bytes 524320 | tf_op jit(solution)/shard_map/ppermute | solution.py:17
  168.2 6.4 copy.187
  205.7 503.7 %while.40 = (s32[]{:T(128)}, f32[3]{0:T(128)S(1)}, f32[3,3]{1,0:T(4,128)S(1)}, f32[3]{0:T(128)S(1)}, s32[]{:T(128)}) while((s32[]{:T(128)}, f32[3]{0:T(128)S(1)}, f32[3,3]{1,0:T(4,128)S(1)}, f32[3]{0:T(128)S(1)}, s32[]{:T(128)}) %tuple.107), condition=%wide.region_26.27_spmd, body=%wide.region_25.26_spmd.sunk | while | flops 113 | bytes 221 | solution.py:154
  207.8 19.4 %collective-permute-done = f32[3]{0:T(128)S(1)} collective-permute-done((f32[3]{0:T(128)S(1)}, f32[3]{0:T(128)S(1)}, u32[]{:S(2)}, u32[]{:S(2)}) %collective-permute-start) | collective-permute-done | bytes 44 | tf_op jit(solution)/shard_map/while/body/eval_jaxpr/ppermute | solution.py:17
  229.3 20.2 %collective-permute-done = f32[3]{0:T(128)S(1)} collective-permute-done((f32[3]{0:T(128)S(1)}, f32[3]{0:T(128)S(1)}, u32[]{:S(2)}, u32[]{:S(2)}) %collective-permute-start) | collective-permute-done | bytes 44 | tf_op jit(solution)/shard_map/while/body/eval_jaxpr/ppermute | solution.py:17
  256.5 20.1 %collective-permute-done = f32[3]{0:T(128)S(1)} collective-permute-done((f32[3]{0:T(128)S(1)}, f32[3]{0:T(128)S(1)}, u32[]{:S(2)}, u32[]{:S(2)}) %collective-permute-start) | collective-permute-done | bytes 44 | tf_op jit(solution)/shard_map/while/body/eval_jaxpr/ppermute | solution.py:17
  283.7 20.9 %collective-permute-done = f32[3]{0:T(128)S(1)} collective-permute-done((f32[3]{0:T(128)S(1)}, f32[3]{0:T(128)S(1)}, u32[]{:S(2)}, u32[]{:S(2)}) %collective-permute-start) | collective-permute-done | bytes 44 | tf_op jit(solution)/shard_map/while/body/eval_jaxpr/ppermute | solution.py:17
  306.6 14.8 %collective-permute-done = f32[3]{0:T(128)S(1)} collective-permute-done((f32[3]{0:T(128)S(1)}, f32[3]{0:T(128)S(1)}, u32[]{:S(2)}, u32[]{:S(2)}) %collective-permute-start) | collective-permute-done | bytes 44 | tf_op jit(solution)/shard_map/while/body/eval_jaxpr/ppermute | solution.py:17
  392.2 5.0 collective-permute-done
  399.3 5.0 collective-permute-done
  406.4 5.0 collective-permute-done
  413.5 5.0 collective-permute-done
  420.6 5.0 collective-permute-done
  427.7 5.0 collective-permute-done
  434.8 5.0 collective-permute-done
  441.9 5.0 collective-permute-done
  449.0 5.0 collective-permute-done
  456.0 5.0 collective-permute-done
  463.1 5.0 collective-permute-done
  470.2 5.0 collective-permute-done
  477.3 5.0 collective-permute-done
  484.4 5.0 collective-permute-done
  491.5 5.0 collective-permute-done
  590.9 5.0 collective-permute-done
  626.4 5.0 collective-permute-done
  713.4 17.6 %all-to-all-start.1 = ((f32[8,2,32]{2,1,0:T(2,128)}), f32[8,2,32]{2,1,0:T(2,128)S(1)}, u32[]{:S(2)}, u32[]{:S(2)}) async-start(f32[8,2,32]{2,1,0:T(2,128)} %bitcast.94), calls=%async_computation.1 | async-start | bytes 16384 | tf_op jit(solution)/shard_map/all_to_all | solution.py:172
  731.0 6.5 all-to-all-done.1
  739.5 62.7 %all_to_all.15 = f32[64,2,4]{2,1,0:T(2,128)S(1)} all-to-all(f32[64,2,4]{2,1,0:T(2,128)S(1)} %bitcast.330), channel_id=1, replica_groups=mesh['seq'=64,'group'=8] {'seq'}, dimensions={0} | all-to-all | bytes 4096 | tf_op jit(solution)/shard_map/all_to_all | solution.py:178
  (537 shorter events, 443.9 us)
Async XLA Ops:
  0.6 78.7 %collective-permute-start.1 = (bf16[256,1024]{1,0:T(8,128)(2,1)}, bf16[256,1024]{1,0:T(8,128)(2,1)}, u32[]{:S(2)}, u32[]{:S(2)}) collective-permute-start(bf16[256,1024]{1,0:T(8,128)(2,1)} %bitcast.321), channel_id=1, source_target_pairs={{0,8},{8,16},{16,24},{24,32},{32,40},{40,48},{48,56},{56,64},{64,7... | collective-permute-start | bytes 1572872 | tf_op jit(solution)/shard_map/ppermute | solution.py:17
  5.2 81.2 %collective-permute-start.2 = (bf16[256,1024]{1,0:T(8,128)(2,1)}, bf16[256,1024]{1,0:T(8,128)(2,1)}, u32[]{:S(2)}, u32[]{:S(2)}) collective-permute-start(bf16[256,1024]{1,0:T(8,128)(2,1)} %bitcast.322), channel_id=1, source_target_pairs={{0,16},{8,24},{16,32},{24,40},{32,48},{40,56},{48,64},{56,72},{64,... | collective-permute-start | bytes 1572872 | tf_op jit(solution)/shard_map/ppermute | solution.py:17
  9.2 83.7 %collective-permute-start.3 = (bf16[256,1024]{1,0:T(8,128)(2,1)}, bf16[256,1024]{1,0:T(8,128)(2,1)}, u32[]{:S(2)}, u32[]{:S(2)}) collective-permute-start(bf16[256,1024]{1,0:T(8,128)(2,1)} %bitcast.323), channel_id=1, source_target_pairs={{0,24},{8,32},{16,40},{24,48},{32,56},{40,64},{48,72},{56,80},{64,... | collective-permute-start | bytes 1572872 | tf_op jit(solution)/shard_map/ppermute | solution.py:17
  12.5 82.5 %collective-permute-start.4 = (bf16[256,1024]{1,0:T(8,128)(2,1)}, bf16[256,1024]{1,0:T(8,128)(2,1)}, u32[]{:S(2)}, u32[]{:S(2)}) collective-permute-start(bf16[256,1024]{1,0:T(8,128)(2,1)} %bitcast.324), channel_id=1, source_target_pairs={{0,32},{8,40},{16,48},{24,56},{32,64},{40,72},{48,80},{56,88},{64,... | collective-permute-start | bytes 1572872 | tf_op jit(solution)/shard_map/ppermute | solution.py:17
  22.8 46.6 %all-to-all-start = ((s32[8,1,32]{2,1,0:T(1,128)}), s32[8,1,32]{2,1,0:T(1,128)S(1)}, u32[]{:S(2)}, u32[]{:S(2)}) async-start(s32[8,1,32]{2,1,0:T(1,128)} %transpose_reshape.3), calls=%async_computation | async-start | bytes 8192 | tf_op jit(solution)/shard_map/all_to_all | solution.py:173
  76.6 27.1 %collective-permute-start.5 = (bf16[256,1024]{1,0:T(8,128)(2,1)}, bf16[256,1024]{1,0:T(8,128)(2,1)S(1)}, u32[]{:S(2)}, u32[]{:S(2)}) collective-permute-start(bf16[256,1024]{1,0:T(8,128)(2,1)} %bitcast.325), channel_id=1, source_target_pairs={{0,40},{8,48},{16,56},{24,64},{32,72},{40,80},{48,88},{56,96},{64,... | collective-permute-start | bytes 1572872 | tf_op jit(solution)/shard_map/ppermute | solution.py:17
  81.2 55.5 %collective-permute-start.6 = (bf16[256,1024]{1,0:T(8,128)(2,1)}, bf16[256,1024]{1,0:T(8,128)(2,1)S(1)}, u32[]{:S(2)}, u32[]{:S(2)}) collective-permute-start(bf16[256,1024]{1,0:T(8,128)(2,1)} %bitcast.326), channel_id=1, source_target_pairs={{0,48},{8,56},{16,64},{24,72},{32,80},{40,88},{48,96},{56,104},{64... | collective-permute-start | bytes 1572872 | tf_op jit(solution)/shard_map/ppermute | solution.py:17
  88.4 77.9 %collective-permute-start.7 = (bf16[256,1024]{1,0:T(8,128)(2,1)S(1)}, bf16[256,1024]{1,0:T(8,128)(2,1)S(1)}, u32[]{:S(2)}, u32[]{:S(2)}) collective-permute-start(bf16[256,1024]{1,0:T(8,128)(2,1)S(1)} %bitcast.327), channel_id=1, source_target_pairs={{0,56},{8,64},{16,72},{24,80},{32,88},{40,96},{48,104},{56,112},{6... | collective-permute-start | bytes 1572872 | tf_op jit(solution)/shard_map/ppermute | solution.py:17
  205.9 21.4 %collective-permute-start = (f32[3]{0:T(128)S(1)}, f32[3]{0:T(128)S(1)}, u32[]{:S(2)}, u32[]{:S(2)}) collective-permute-start(f32[3]{0:T(128)S(1)} %fusion.179), channel_id=1, source_target_pairs={{8,0},{16,8},{24,16},{32,24},{40,32},{48,40},{56,48},{64,56},{72,6... | collective-permute-start | bytes 44 | tf_op jit(solution)/shard_map/while/body/eval_jaxpr/ppermute | solution.py:17
  227.3 22.1 %collective-permute-start = (f32[3]{0:T(128)S(1)}, f32[3]{0:T(128)S(1)}, u32[]{:S(2)}, u32[]{:S(2)}) collective-permute-start(f32[3]{0:T(128)S(1)} %fusion.179), channel_id=1, source_target_pairs={{8,0},{16,8},{24,16},{32,24},{40,32},{48,40},{56,48},{64,56},{72,6... | collective-permute-start | bytes 44 | tf_op jit(solution)/shard_map/while/body/eval_jaxpr/ppermute | solution.py:17
  254.6 22.0 %collective-permute-start = (f32[3]{0:T(128)S(1)}, f32[3]{0:T(128)S(1)}, u32[]{:S(2)}, u32[]{:S(2)}) collective-permute-start(f32[3]{0:T(128)S(1)} %fusion.179), channel_id=1, source_target_pairs={{8,0},{16,8},{24,16},{32,24},{40,32},{48,40},{56,48},{64,56},{72,6... | collective-permute-start | bytes 44 | tf_op jit(solution)/shard_map/while/body/eval_jaxpr/ppermute | solution.py:17
  281.8 22.8 %collective-permute-start = (f32[3]{0:T(128)S(1)}, f32[3]{0:T(128)S(1)}, u32[]{:S(2)}, u32[]{:S(2)}) collective-permute-start(f32[3]{0:T(128)S(1)} %fusion.179), channel_id=1, source_target_pairs={{8,0},{16,8},{24,16},{32,24},{40,32},{48,40},{56,48},{64,56},{72,6... | collective-permute-start | bytes 44 | tf_op jit(solution)/shard_map/while/body/eval_jaxpr/ppermute | solution.py:17
  304.7 16.7 %collective-permute-start = (f32[3]{0:T(128)S(1)}, f32[3]{0:T(128)S(1)}, u32[]{:S(2)}, u32[]{:S(2)}) collective-permute-start(f32[3]{0:T(128)S(1)} %fusion.179), channel_id=1, source_target_pairs={{8,0},{16,8},{24,16},{32,24},{40,32},{48,40},{56,48},{64,56},{72,6... | collective-permute-start | bytes 44 | tf_op jit(solution)/shard_map/while/body/eval_jaxpr/ppermute | solution.py:17
  390.3 7.0 collective-permute-start
  397.3 7.0 collective-permute-start
  404.4 7.0 collective-permute-start
  411.5 7.0 collective-permute-start
  418.6 7.0 collective-permute-start
  425.7 7.0 collective-permute-start
  432.8 7.0 collective-permute-start
  439.9 7.0 collective-permute-start
  447.0 7.0 collective-permute-start
  454.1 7.0 collective-permute-start
  461.2 7.0 collective-permute-start
  468.3 7.0 collective-permute-start
  475.4 7.0 collective-permute-start
  482.5 7.0 collective-permute-start
  489.6 7.0 collective-permute-start
  496.7 7.0 collective-permute-start
  588.9 7.0 collective-permute-start
  624.4 7.0 collective-permute-start
  713.4 24.2 %all-to-all-start.1 = ((f32[8,2,32]{2,1,0:T(2,128)}), f32[8,2,32]{2,1,0:T(2,128)S(1)}, u32[]{:S(2)}, u32[]{:S(2)}) async-start(f32[8,2,32]{2,1,0:T(2,128)} %bitcast.94), calls=%async_computation.1 | async-start | bytes 16384 | tf_op jit(solution)/shard_map/all_to_all | solution.py:172
  (82 other events, 3091.0 us)
where the time goes:
time: 808 us; the launch traced here: 804 us
  waiting for transfers between devices  448 us (55%)
  starting transfers between devices  177 us (22%)
  local copies, waits for them, and re-layouts  66.3 us (8%)
  blocking collectives  62.7 us (8%)
  other arithmetic  25.2 us (3%)
  matrix products  19.7 us (2%)
    ppermute x70, waiting for transfers between devices, from_behind(): lax.ppermute(value, axis, [(source, source + steps) for source in range(i...  442 us
    ppermute x70, starting transfers between devices, from_behind(): lax.ppermute(value, axis, [(source, source + steps) for source in range(i...  150 us
    all_to_all x1, blocking collectives, shards(): lax.all_to_all(second, 'seq', split_axis=0, concat_axis=0, tiled=True)  62.7 us
    all_to_all x1, starting transfers between devices, shards(): lax.all_to_all(sectioned, 'group', split_axis=0, concat_axis=0, tiled=True)  17.6 us
    unnamed x106, local copies, waits for them, and re-layouts  16.9 us
  transfers between devices with their start and end apart: 72, of which 67 were waited for; matrix products, arithmetic and copies ran while one was open for 7% of the time, Pallas kernels for 0%

commit v1 on v0

v1 whole, which is shorter than its diff:
```python
import math

import jax
import jax.numpy as jnp
from jax import lax
from jax.experimental import pallas as pl
from jax.experimental.pallas import tpu as pltpu
from jax.sharding import PartitionSpec as P

HD = 128
BLK = 128
TOK = 256
KVH = 4
HEADS = 32
PER = HEADS // KVH
HALF = KVH * HD
LIST = 8
MSG = TOK + HEADS // 2
TRACE = 0.995
LOG_TRACE = math.log(TRACE)
TO_LOG2 = HD ** -0.5 * math.log2(math.e)
LOW = -1e30
F32 = jnp.float32
BF16 = jnp.bfloat16

NT = (((1,), (1,)), ((), ()))
SMEM = pl.BlockSpec(memory_space=pltpu.SMEM)
VMEM = pl.BlockSpec(memory_space=pltpu.VMEM)


def iota(shape, dim):
    return lax.broadcasted_iota(jnp.int32, shape, dim)


def three(x):
    first = x.astype(BF16)
    rest = x - first.astype(F32)
    second = rest.astype(BF16)
    third = (rest - second.astype(F32)).astype(BF16)
    return first, second, third


def message_kernel(kv_ref, dir_ref, out_ref):
    out_ref[0:TOK, :] = kv_ref[:, 0:HALF]
    direction = dir_ref[...]
    head = iota((HEADS, HD), 0)
    zero = jnp.zeros_like(direction)
    spread = jnp.concatenate(
        [jnp.where(head // PER == k, direction, zero) for k in range(KVH)], axis=1
    )
    read = lax.dot_general(
        spread, kv_ref[:, HALF:], NT, preferred_element_type=F32
    ).astype(BF16)
    out_ref[TOK:MSG, 0:TOK] = read[0 : HEADS // 2]
    out_ref[TOK:MSG, TOK:HALF] = read[HEADS // 2 :]


def message(kv, direction):
    return pl.pallas_call(
        message_kernel,
        out_shape=jax.ShapeDtypeStruct((MSG, HALF), BF16),
        in_specs=[VMEM, VMEM],
        out_specs=VMEM,
        cost_estimate=pl.CostEstimate(
            flops=2 * TOK * HALF * HEADS, bytes_accessed=800_000, transcendentals=0
        ),
        name="message",
    )(kv, direction)


def weights_kernel(place_ref, rew_ref, turn_ref, base_ref, dest_ref, m_ref, oh_ref, row_ref, col_ref):
    shard = place_ref[0]
    sub, lane = iota((TOK, TOK), 0), iota((TOK, TOK), 1)
    diag = sub == lane

    def column(row):
        return jnp.sum(jnp.where(diag, row, 0.0), axis=1, keepdims=True)

    spot = iota((1, TOK), 1)
    begins = (turn_ref[...] == 1) | ((shard == 0) & (spot == 0))
    start_row = jnp.where(begins, 1.0, 0.0)
    start_col = column(start_row)
    c_row = jnp.sum(jnp.where(sub <= lane, start_col, 0.0), axis=0, keepdims=True)
    c_col = jnp.sum(jnp.where(lane <= sub, start_row, 0.0), axis=1, keepdims=True)
    rewards = column(rew_ref[...])
    base = column(base_ref[...])
    gap = c_col - c_row
    opens = start_col > 0.5
    m = jnp.where((sub > lane) & opens, (1.0 - TRACE) * jnp.exp((gap - 1.0) * LOG_TRACE), 0.0)
    m_ref[...] = m
    decay = jnp.where(sub >= lane, jnp.exp(gap * LOG_TRACE), 0.0)
    known = jnp.sum(decay * rewards + m * base, axis=0, keepdims=True)
    total = jnp.sum(start_row, axis=1, keepdims=True)
    b_col = jnp.where(opens, (1.0 - TRACE) * jnp.exp((c_col - 1.0) * LOG_TRACE), 0.0)
    col_ref[...] = jnp.broadcast_to(b_col, (TOK, HD))
    b_known = jnp.sum(b_col * base + jnp.exp(c_col * LOG_TRACE) * rewards, axis=0, keepdims=True)
    dest = dest_ref[...]
    to_group = lax.rem(dest, 8).astype(F32)
    to_seq = (dest // 8).astype(F32)
    group_col = column(to_group)
    rank = jnp.sum(jnp.where((group_col == to_group) & (lane < sub), 1.0, 0.0), axis=1, keepdims=True)
    slot = (group_col * 32.0 + rank).astype(jnp.int32)
    oh_ref[...] = jnp.where(slot == lane, 1.0, 0.0).astype(BF16)
    wide = (1, TOK)
    rows = [
        base_ref[...],
        known,
        jnp.exp((total - c_row) * LOG_TRACE),
        to_seq,
        jnp.broadcast_to(jnp.exp(total * LOG_TRACE), wide),
        jnp.broadcast_to(b_known, wide),
        jnp.zeros(wide, F32),
        jnp.zeros(wide, F32),
    ]
    row_ref[...] = jnp.concatenate(rows, axis=0)


def weights(place, rewards, turns, base, dest):
    return pl.pallas_call(
        weights_kernel,
        out_shape=(
            jax.ShapeDtypeStruct((TOK, TOK), F32),
            jax.ShapeDtypeStruct((TOK, TOK), BF16),
            jax.ShapeDtypeStruct((8, TOK), F32),
            jax.ShapeDtypeStruct((TOK, HD), F32),
        ),
        in_specs=[SMEM, VMEM, VMEM, VMEM, VMEM],
        out_specs=(VMEM, VMEM, VMEM, VMEM),
        cost_estimate=pl.CostEstimate(flops=2_000_000, bytes_accessed=600_000, transcendentals=200_000),
        name="weights",
    )(place, rewards, turns, base, dest)


def attend_kernel(slots, has_own, place_ref, list_ref, q_ref, *rest):
    count = len(slots)
    msgs, out_ref, keys, reads, scores, found = rest[:count], *rest[count:]
    shard = place_ref[0]
    core = lax.rem(shard, 2)
    for i, msg in enumerate(msgs):
        for half in range(2):
            keys[2 * i + half] = msg[half * BLK : (half + 1) * BLK, :]
            for part in range(2):
                at = part * TOK + half * BLK
                reads[2 * i + half, part * 16 : (part + 1) * 16, :] = msg[
                    TOK:MSG, at : at + BLK
                ].astype(F32)
    for qb in range(2):
        block = shard * 2 + qb
        n = jnp.int32(0)
        entries = [list_ref[qb, j] for j in range(LIST)]
        for j in range(LIST):
            found[qb, j] = 0
        for j in range(LIST):
            entry = entries[j]
            use = entry < block
            for i in range(j):
                use = use & (entries[i] != entry)
            back = shard - entry // 2
            even = lax.rem(back, 2) == 0
            slot = jnp.where(even, back // 2, 4 + lax.rem(back // 2 + 1 - core, 4))
            local = jnp.int32(0)
            here = jnp.bool_(False)
            for i, s in enumerate(slots):
                hit = slot == s
                local = jnp.where(hit, 2 * i, local)
                here = here | hit
            found[qb, jnp.minimum(n, LIST - 1)] = jnp.where(
                use & here, local + lax.rem(entry, 2), found[qb, jnp.minimum(n, LIST - 1)]
            )
            n = n + jnp.where(use & here, 1, 0)
        found[qb, LIST] = n

    lane = iota((BLK, BLK), 1)
    causal = lane <= iota((BLK, BLK), 0)
    out_ref[...] = jnp.zeros_like(out_ref)

    def step(index, carry):
        qb, k = index // KVH, lax.rem(index, KVH)
        rows = pl.ds(pl.multiple_of(qb * BLK, BLK), BLK)
        n = found[qb, LIST]
        head_keys = pl.ds(pl.multiple_of(k * HD, HD), HD)

        def run(pairs):
            heads = [
                q_ref[rows, pl.ds(pl.multiple_of(k * (PER * HD) + g * HD, HD), HD)] for g in range(PER)
            ]
            query = jnp.concatenate(heads, axis=0)
            columns = []
            if has_own:
                own = qb + 2 * slots.index(0)
                columns.append(own)
                scores[:, 0:BLK] = lax.dot_general(
                    query, keys[own, :, head_keys], NT, preferred_element_type=F32
                )
            for j in range(pairs):
                two = [found[qb, 2 * j], found[qb, 2 * j + 1]]
                both = jnp.concatenate([keys[s, :, head_keys] for s in two], axis=0)
                at = len(columns) * BLK
                scores[:, at : at + 2 * BLK] = lax.dot_general(
                    query, both, NT, preferred_element_type=F32
                )
                columns += two
            spare = jnp.where(n == 2 * pairs, 0.0, LOW)
            acc = [jnp.zeros((BLK, BLK), F32)] * 3
            for g in range(PER):
                top = None
                for j in range(len(columns)):
                    s = scores[g * BLK : (g + 1) * BLK, j * BLK : (j + 1) * BLK]
                    if has_own and j == 0:
                        s = jnp.where(causal, s, LOW)
                    elif j == len(columns) - 1:
                        s = s + spare
                    top = s if top is None else jnp.maximum(top, s)
                peak = jnp.max(top, axis=1, keepdims=True) * TO_LOG2
                total = None
                for j, slot in enumerate(columns):
                    s = scores[g * BLK : (g + 1) * BLK, j * BLK : (j + 1) * BLK]
                    if has_own and j == 0:
                        s = jnp.where(causal, s, LOW)
                    elif j == len(columns) - 1:
                        s = s + spare
                    p = jnp.exp2(s * TO_LOG2 - peak)
                    v = p * reads[slot, pl.ds(k * PER + g, 1), :]
                    total = p if total is None else total + p
                    summed = v if j == 0 else summed + v
                mine = lane == k * PER + g
                for f, x in enumerate(
                    (peak, jnp.sum(total, axis=1, keepdims=True), jnp.sum(summed, axis=1, keepdims=True))
                ):
                    acc[f] = jnp.where(mine, x, acc[f])
            for f in range(3):
                out_ref[f, rows, :] += acc[f]

        def nothing():
            mine = (lane >= k * PER) & (lane < (k + 1) * PER)
            out_ref[0, rows, :] += jnp.where(mine, LOW, 0.0)

        for pairs in range(LIST // 2 + 1):
            if 2 * pairs - 1 > 4 * len(slots):
                continue

            @pl.when((n + 1) // 2 == pairs)
            def _(pairs=pairs):
                if pairs == 0 and not has_own:
                    nothing()
                else:
                    run(pairs)

        return carry

    lax.fori_loop(0, 2 * KVH, step, 0)


def attend(slots, has_own, place, lists, q, msgs):
    blocks = 2 * len(slots)
    return pl.pallas_call(
        lambda *refs: attend_kernel(slots, has_own, *refs),
        out_shape=jax.ShapeDtypeStruct((3, TOK, HD), F32),
        in_specs=[SMEM, SMEM, VMEM] + [VMEM] * len(slots),
        out_specs=VMEM,
        scratch_shapes=[
            pltpu.VMEM((blocks, BLK, HALF), BF16),
            pltpu.VMEM((blocks, HEADS, BLK), F32),
            pltpu.VMEM((PER * BLK, (LIST + 1) * BLK), F32),
            pltpu.SMEM((2, LIST + 1), jnp.int32),
        ],
        compiler_params=pltpu.CompilerParams(vmem_limit_bytes=32 * 1024 * 1024),
        cost_estimate=pl.CostEstimate(
            flops=2 * 2 * HEADS * BLK * HD * BLK * 5, bytes_accessed=4_000_000, transcendentals=5_000_000
        ),
        name="attend",
    )(place, lists, q, *msgs)


def values_kernel(parts, *refs):
    partials, (m_ref, oh_ref, row_ref, col_ref, val_ref, pay_ref) = refs[:parts], refs[parts:]
    top = partials[0][0]
    for x in partials[1:]:
        top = jnp.maximum(top, x[0])
    total = summed = 0.0
    for x in partials:
        w = jnp.exp2(x[0] - top)
        total = total + x[1] * w
        summed = summed + x[2] * w
    lane = iota((TOK, HD), 1)
    share = jnp.where(lane < HEADS, summed / jnp.where(lane < HEADS, total, 1.0), 0.0)
    att = jnp.sum(share, axis=1, keepdims=True)
    diag = iota((TOK, TOK), 0) == iota((TOK, TOK), 1)
    fields = row_ref[...]
    value = fields[0:1] + jnp.sum(jnp.where(diag, att, 0.0), axis=0, keepdims=True)
    val_ref[...] = value
    local = fields[1:2] + jnp.sum(m_ref[...] * att, axis=0, keepdims=True)
    b = jnp.sum(col_ref[...] * att, axis=0, keepdims=True)
    b = fields[5:6] + jnp.concatenate([b, b], axis=1)
    rows = jnp.concatenate([value, local, fields[2:5], b, fields[6:8]], axis=0)
    split = jnp.concatenate(three(rows), axis=0)
    moved = jnp.dot(split, oh_ref[...], preferred_element_type=F32)
    moved = moved[0:8] + moved[8:16] + moved[16:24]
    pay_ref[...] = jnp.zeros_like(pay_ref)
    for g in range(8):
        pay_ref[g, :, 0:32] = moved[:, g * 32 : (g + 1) * 32]


def token_part(partials, m, onehot, rows, cols):
    return pl.pallas_call(
        lambda *refs: values_kernel(len(partials), *refs),
        out_shape=(
            jax.ShapeDtypeStruct((1, TOK), F32),
            jax.ShapeDtypeStruct((8, 8, HD), F32),
        ),
        in_specs=[VMEM] * (len(partials) + 4),
        out_specs=(VMEM, VMEM),
        cost_estimate=pl.CostEstimate(flops=2_000_000, bytes_accessed=1_500_000, transcendentals=65_000),
        name="token_part",
    )(*partials, m, onehot, rows, cols)


def sort_kernel(in_ref, out_ref):
    seqs = iota((64, HD), 0)
    lane = iota((64, HD), 1)
    before = jnp.where(iota((HD, HD), 0) < iota((HD, HD), 1), 1.0, 0.0).astype(BF16)
    ahead = jnp.zeros((64, 1), F32)
    onehots, fields = [], []
    known = jnp.zeros((1, HD), F32)
    lane_row = iota((1, HD), 1)
    zero = jnp.zeros((1, HD), F32)
    for g in range(8):
        x = in_ref[g]
        tag = x[3:4].astype(jnp.int32)
        hit = (seqs == tag) & (lane < 32)
        one = jnp.where(hit, 1.0, 0.0)
        onehot = one.astype(BF16)
        counts = jnp.dot(onehot, before, preferred_element_type=F32) + ahead
        rank = jnp.sum(one * counts, axis=0, keepdims=True)
        ahead = ahead + jnp.sum(one, axis=1, keepdims=True)
        group = jnp.full((1, HD), float(g), F32)
        rows = [
            jnp.where(rank == float(r), f, zero)
            for f in (x[0:1], x[1:2], x[2:3], group)
            for r in range(4)
        ]
        onehots.append(onehot)
        fields.append(jnp.concatenate(rows, axis=0))
        known = jnp.where(lane_row == 16 + g, x[4:5, 0:1], known)
        known = jnp.where(lane_row == 24 + g, x[5:6, 0:1], known)
    table = jnp.concatenate(fields, axis=1)
    table = jnp.concatenate([table, jnp.zeros((HD - 16, 8 * HD), F32)], axis=0)
    onehot = jnp.concatenate(onehots, axis=1)
    moved = 0.0
    for part in three(table):
        moved = moved + lax.dot_general(onehot, part, NT, preferred_element_type=F32)
    out_ref[...] = moved + known


def sort_part(received):
    return pl.pallas_call(
        sort_kernel,
        out_shape=jax.ShapeDtypeStruct((64, HD), F32),
        in_specs=[VMEM],
        out_specs=VMEM,
        cost_estimate=pl.CostEstimate(flops=10_000_000, bytes_accessed=70_000, transcendentals=0),
        name="sort_part",
    )(received)


def finish_kernel(in_ref, adv_ref, ret_ref):
    x = in_ref[...]
    seqs = iota((64, HD), 0)
    lane = iota((64, HD), 1)
    factor = x
    offset = pltpu.roll(x, HD - 8, axis=1)
    span = 1
    while span < 64:
        inside = seqs < 64 - span
        next_factor = jnp.where(inside, pltpu.roll(factor, 64 - span, axis=0), 1.0)
        next_offset = jnp.where(inside, pltpu.roll(offset, 64 - span, axis=0), 0.0)
        offset = offset + factor * next_offset
        factor = factor * next_factor
        span *= 2
    incoming = jnp.where(seqs < 63, pltpu.roll(offset, 63, axis=0), 0.0)
    wide = (64, TOK)
    spot = iota(wide, 1) - 4 * iota(wide, 0)
    adv = jnp.zeros(wide, F32)
    ret = jnp.zeros(wide, F32)
    for r in range(4):
        group = x[:, 12 + r : 13 + r].astype(jnp.int32)
        entry = jnp.sum(jnp.where(lane == group + 16, incoming, 0.0), axis=1, keepdims=True)
        returns = x[:, 4 + r : 5 + r] + x[:, 8 + r : 9 + r] * entry
        advantage = returns - x[:, r : r + 1]
        adv = jnp.where(spot == r, advantage, adv)
        ret = jnp.where(spot == r, returns, ret)
    adv_ref[...] = jnp.sum(adv, axis=0, keepdims=True)
    ret_ref[...] = jnp.sum(ret, axis=0, keepdims=True)


def finish(arrived):
    return pl.pallas_call(
        finish_kernel,
        out_shape=(jax.ShapeDtypeStruct((1, TOK), F32),) * 2,
        in_specs=[VMEM],
        out_specs=(VMEM, VMEM),
        cost_estimate=pl.CostEstimate(flops=500_000, bytes_accessed=40_000, transcendentals=0),
        name="finish",
    )(arrived)


def forward(value, distance, count):
    return lax.ppermute(value, "seq", [(s, s + distance) for s in range(count - distance)])


def swap(value, count):
    return lax.ppermute(value, "seq", [(s, s ^ 1) for s in range(count)])


def shards(queries, keys_values, block_list, value_dir, base_values, rewards, turn_start, actor_shard):
    count = lax.axis_size("seq")
    shard = lax.axis_index("seq").astype(jnp.int32)
    place = shard[None]
    own = message(keys_values[0], value_dir.reshape(HEADS, HD))
    a = forward(own, 2, count)
    b = forward(a, 2, count)
    wa = swap(a, count)
    c = forward(b, 2, count)
    wb = swap(b, count)
    wc = swap(c, count)
    far = [(s, s + 1) for s in range(1, count - 1, 2)]
    near = [(s, s + 1) for s in range(0, count, 2)]
    x = lax.ppermute(jnp.where(shard % 2 == 0, own, c), "seq", far + near)
    m, onehot, rows, cols = weights(place, rewards, turn_start, base_values, actor_shard)
    q, lists = queries[0], block_list[0]
    part = attend((0, 1, 2, 3, 4, 5, 6, 7), True, place, lists, q, (own, a, b, c, x, wa, wb, wc))
    values, payload = token_part((part,), m, onehot, rows, cols)
    received = lax.all_to_all(payload, "group", split_axis=0, concat_axis=0, tiled=True)
    arranged = sort_part(received)
    arrived = lax.all_to_all(arranged, "seq", split_axis=0, concat_axis=0, tiled=True)
    advantage, returns = finish(arrived)
    return values, advantage.reshape(TOK), returns.reshape(TOK)


def solution(mesh):
    placed = (
        P("group", "seq", None),
        P("group", "seq", None),
        P("group", "seq", None),
        P(),
        P("group", "seq"),
        P("group", "seq"),
        P("group", "seq"),
        P("group", "seq"),
    )
    return jax.shard_map(
        shards,
        mesh=mesh,
        in_specs=placed,
        out_specs=(P("group", "seq"), P(("seq", "group")), P(("seq", "group"))),
        check_vma=False,
    )
```

time: 808 us -> 106 us (0.13)
  waiting for transfers between devices: 448 us -> 7.24 us
  starting transfers between devices: 177 us -> 28.8 us
  local copies, waits for them, and re-layouts: 66.3 us -> 3.95 us
  other arithmetic: 25.2 us -> 0.04 us
  matrix products: 19.7 us -> 0 us
  Pallas kernels: 0 us -> 17.1 us
  blocking collectives: 62.7 us -> 47.3 us
    ppermute x70 -> x7, waiting for transfers between devices: 442 us -> 7.24 us  [the longest x3 7.23 us: forward(): lax.ppermute(value, 'seq', [(s, s + distance) for s in range(count - dist...]
    ppermute x70 -> x7, starting transfers between devices: 150 us -> 28.8 us  [the longest x3 14 us: forward(): lax.ppermute(value, 'seq', [(s, s + distance) for s in range(count - dist...]
    all_to_all x2 -> x0, starting transfers between devices: 27.7 us -> none  [the longest x1 17.6 us: shards(): lax.all_to_all(sectioned, 'group', split_axis=0, concat_axis=0, tiled=True)]
    dot_general x86 -> x0, matrix products: 19.7 us -> none  [the longest x63 8.09 us: relay_step(): jnp.dot(summary_map, incoming, precision=lax.Precision.HIGHEST)]
    pallas_call x0 -> x6, Pallas kernels: none -> 17.1 us  [the longest x1 7.45 us: attend(): pl.pallas_call(lambda *refs: attend_kernel(slots, has_own, *refs), out_sh...]
    all_to_all x1 -> x2, blocking collectives: 62.7 us -> 47.3 us  [the longest x1 30.2 us: shards(): lax.all_to_all(arranged, 'seq', split_axis=0, concat_axis=0, tiled=True)]
    slice x53 -> x0, local copies, waits for them, and re-layouts: 14.2 us -> none  [the longest x39 3.45 us: shards(): lax.associative_scan(compose, (maps[::-1], offsets[::-1]))]
    unnamed x106 -> x8, local copies, waits for them, and re-layouts: 16.9 us -> 3.95 us
  transfers between devices with their start and end apart: 72 -> 7, of which waited for: 67 -> 2; matrix products, arithmetic and copies ran while one was open for 7% -> 0% of each run, Pallas kernels for 0% -> 2%
where the time goes in v1:
time: 106 us; the launch traced here: 105 us
  blocking collectives  47.3 us (45%)
  starting transfers between devices  28.8 us (27%)
  Pallas kernels  17.1 us (16%)
  waiting for transfers between devices  7.24 us (7%)
  local copies, waits for them, and re-layouts  3.95 us (4%)
    all_to_all x1, blocking collectives, shards(): lax.all_to_all(arranged, 'seq', split_axis=0, concat_axis=0, tiled=True)  30.2 us
    all_to_all x1, blocking collectives, shards(): lax.all_to_all(payload, 'group', split_axis=0, concat_axis=0, tiled=True)  17.2 us
    ppermute x3, starting transfers between devices, forward(): lax.ppermute(value, 'seq', [(s, s + distance) for s in range(count - dist...  14 us
    ppermute x3, starting transfers between devices, swap(): return lax.ppermute(value, 'seq', [(s, s ^ 1) for s in range(count)])  9.76 us
    pallas_call x1, Pallas kernels, attend(): pl.pallas_call(lambda *refs: attend_kernel(slots, has_own, *refs), out_sh...  7.45 us
    ppermute x3, waiting for transfers between devices, forward(): lax.ppermute(value, 'seq', [(s, s + distance) for s in range(count - dist...  7.23 us
    ppermute x1, starting transfers between devices, shards(): x = lax.ppermute(jnp.where(shard % 2 == 0, own, c), 'seq', far + near)  5.1 us
    unnamed x8, local copies, waits for them, and re-layouts  3.95 us
  transfers between devices with their start and end apart: 7, of which 2 were waited for; matrix products, arithmetic and copies ran while one was open for 0% of the time, Pallas kernels for 2%

profile of v1, /device:TPU:1, one launch (start us, length us, event | category | flops | bytes accessed | tf_op | source)
XLA Modules:
  0.0 105.3 jit_solution(12536156817745654355)
XLA Ops:
  0.6 1.9 %message.1.refs_3_ = bf16[272,512]{1,0:T(8,128)(2,1)} custom-call(bf16[256,1024]{1,0:T(8,128)(2,1)} %bitcast.13, bf16[32,128]{1,0:T(8,128)(2,1)} %bitcast.16), custom_call_target="tpu_custom_call" | custom-call | flops 8388608 | bytes 800000 | tf_op jit(solution)/shard_map/message/pallas_call | solution.py:59
  2.6 4.0 %collective-permute-start = (bf16[272,512]{1,0:T(8,128)(2,1)}, bf16[272,512]{1,0:T(8,128)(2,1)S(1)}, u32[]{:S(2)}, u32[]{:S(2)}) collective-permute-start(bf16[272,512]{1,0:T(8,128)(2,1)} %message.1.refs_3_), channel_id=1, source_target_pairs={{0,16},{8,24},{16,32},{24,40},{32,48},{40,56},{48,64},{56,72},{64,... | collective-permute-start | bytes 835592 | tf_op jit(solution)/shard_map/ppermute | solution.py:408
  6.6 3.8 %collective-permute-done.refs_4_ = bf16[272,512]{1,0:T(8,128)(2,1)S(1)} collective-permute-done((bf16[272,512]{1,0:T(8,128)(2,1)}, bf16[272,512]{1,0:T(8,128)(2,1)S(1)}, u32[]{:S(2)}, u32[]{:S(2)}) %collective-permute-start) | collective-permute-done | bytes 278560 | tf_op jit(solution)/shard_map/ppermute | solution.py:408
  10.4 5.0 %collective-permute-start.1 = (bf16[272,512]{1,0:T(8,128)(2,1)S(1)}, bf16[272,512]{1,0:T(8,128)(2,1)S(1)}, u32[]{:S(2)}, u32[]{:S(2)}) collective-permute-start(bf16[272,512]{1,0:T(8,128)(2,1)S(1)} %collective-permute-done.refs_4_), channel_id=1, source_target_pairs={{0,16},{8,24},{16,32},{24,40},{32,48},{40,56},{48,64},{56,72},{64,... | collective-permute-start | bytes 835592 | tf_op jit(solution)/shard_map/ppermute | solution.py:408
  15.4 3.5 %collective-permute-done.1.refs_5_ = bf16[272,512]{1,0:T(8,128)(2,1)S(1)} collective-permute-done((bf16[272,512]{1,0:T(8,128)(2,1)S(1)}, bf16[272,512]{1,0:T(8,128)(2,1)S(1)}, u32[]{:S(2)}, u32[]{:S(2)}) %collective-permute-start.1) | collective-permute-done | bytes 278560 | tf_op jit(solution)/shard_map/ppermute | solution.py:408
  18.9 4.9 %collective-permute-start.2 = (bf16[272,512]{1,0:T(8,128)(2,1)S(1)}, bf16[272,512]{1,0:T(8,128)(2,1)S(1)}, u32[]{:S(2)}, u32[]{:S(2)}) collective-permute-start(bf16[272,512]{1,0:T(8,128)(2,1)S(1)} %collective-permute-done.1.refs_5_), channel_id=1, source_target_pairs={{0,16},{8,24},{16,32},{24,40},{32,48},{40,56},{48,64},{56,72},{64,... | collective-permute-start | bytes 835592 | tf_op jit(solution)/shard_map/ppermute | solution.py:408
  23.8 5.9 %collective-permute-start.4 = (bf16[272,512]{1,0:T(8,128)(2,1)S(1)}, bf16[272,512]{1,0:T(8,128)(2,1)S(1)}, u32[]{:S(2)}, u32[]{:S(2)}) collective-permute-start(bf16[272,512]{1,0:T(8,128)(2,1)S(1)} %collective-permute-done.refs_4_), channel_id=1, source_target_pairs={{0,8},{8,0},{16,24},{24,16},{32,40},{40,32},{48,56},{56,48},{64,72... | collective-permute-start | bytes 835592 | tf_op jit(solution)/shard_map/ppermute | solution.py:412
  29.8 1.9 %collective-permute-start.5 = (bf16[272,512]{1,0:T(8,128)(2,1)S(1)}, bf16[272,512]{1,0:T(8,128)(2,1)S(1)}, u32[]{:S(2)}, u32[]{:S(2)}) collective-permute-start(bf16[272,512]{1,0:T(8,128)(2,1)S(1)} %collective-permute-done.1.refs_5_), channel_id=1, source_target_pairs={{0,8},{8,0},{16,24},{24,16},{32,40},{40,32},{48,56},{56,48},{64,72... | collective-permute-start | bytes 835592 | tf_op jit(solution)/shard_map/ppermute | solution.py:412
  31.7 0.0 collective-permute-done.2.refs_6_
  31.7 5.1 %collective-permute-start.3 = (bf16[272,512]{1,0:T(8,128)(2,1)S(1)}, bf16[272,512]{1,0:T(8,128)(2,1)S(1)}, u32[]{:S(2)}, u32[]{:S(2)}) collective-permute-start(bf16[272,512]{1,0:T(8,128)(2,1)S(1)} %broadcast_select_fusion), channel_id=1, source_target_pairs={{8,16},{24,32},{40,48},{56,64},{72,80},{88,96},{104,112},{120,128}... | collective-permute-start | bytes 835592 | tf_op jit(solution)/shard_map/ppermute | solution.py:428
  36.9 1.9 %collective-permute-start.6 = (bf16[272,512]{1,0:T(8,128)(2,1)S(1)}, bf16[272,512]{1,0:T(8,128)(2,1)S(1)}, u32[]{:S(2)}, u32[]{:S(2)}) collective-permute-start(bf16[272,512]{1,0:T(8,128)(2,1)S(1)} %collective-permute-done.2.refs_6_), channel_id=1, source_target_pairs={{0,8},{8,0},{16,24},{24,16},{32,40},{40,32},{48,56},{56,48},{64,72... | collective-permute-start | bytes 835592 | tf_op jit(solution)/shard_map/ppermute | solution.py:412
  38.8 1.9 %weights.1 = (f32[256,256]{1,0:T(8,128)}, bf16[256,256]{1,0:T(8,128)(2,1)}, f32[8,256]{1,0:T(8,128)}, f32[256,128]{1,0:T(8,128)}) custom-call(s32[1]{0:T(128)} %bitcast.refs_0_.place_ref, f32[1,256]{1,0:T(1,128)} %rew_ref.1, s32[1,256]{1,0:T(1,128)} %turn_ref.1, f32[1,256]{1,0:T(1,128)} %base_ref.1, s32[1,256]{1,0:T(1,128)} %dest_ref.1), custom_call_target="tpu_custom_call" | custom-call | flops 2000000 | bytes 600000 | tf_op jit(solution)/shard_map/weights/pallas_call | solution.py:119
  40.7 0.0 collective-permute-done.4.refs_8_
  40.7 0.0 collective-permute-done.5.refs_9_
  40.7 0.0 collective-permute-done.3.refs_7_
  40.7 0.0 collective-permute-done.6.refs_10_
  40.7 0.0 copy-start
  40.7 0.9 copy-done
  41.7 0.0 copy-start.2
  41.7 1.6 %copy-done.2 = bf16[1,256,4096]{2,1,0:T(8,128)(2,1)S(1)} copy-done((bf16[1,256,4096]{2,1,0:T(8,128)(2,1)S(1)}, bf16[1,256,4096]{2,1,0:T(8,128)(2,1)}, u32[]{:S(2)}) %copy-start.2) | copy-done | bytes 2097176
  43.3 0.0 copy-start.3
  43.3 0.7 copy-done.3
  43.9 7.4 %attend.1.refs_0_ = f32[3,256,128]{2,1,0:T(8,128)S(1)} custom-call(s32[1]{0:T(128)} %bitcast.refs_0_.place_ref, s32[2,8]{1,0:T(2,128)S(1)} %bitcast.12, bf16[256,4096]{1,0:T(8,128)(2,1)S(1)} %bitcast.11, bf16[272,512]{1,0:T(8,128)(2,1)S(1)} %copy-done, bf16[272,512]{1,0:T(8,128)(2,1)S(1)} %collective-permute-done.refs_4_, ...), custom_call_target="tpu_custom_call" | custom-call | flops 1342177280 | bytes 4000000 | tf_op jit(solution)/shard_map/attend/pallas_call | solution.py:256
  51.4 0.0 copy-start.1
  51.4 0.7 copy-done.1
  52.1 2.1 %token_part.1 = (f32[1,256]{1,0:T(1,128)}, f32[8,8,128]{2,1,0:T(8,128)}) custom-call(f32[3,256,128]{2,1,0:T(8,128)} %copy-done.1, f32[256,256]{1,0:T(8,128)} %get-tuple-element.11.refs_1_, bf16[256,256]{1,0:T(8,128)(2,1)} %get-tuple-element.12.refs_2_, f32[8,256]{1,0:T(8,128)} %get-tuple-element.13.refs_3_, f32[256,128]{1,0:T(8,128)} %get-tuple-element.14.refs_4_), custom_call_target="tpu_custom_call" | custom-call | flops 2000000 | bytes 1500000 | tf_op jit(solution)/shard_map/token_part/pallas_call | solution.py:305
  54.2 17.2 %all_to_all.16.in_ref = f32[8,8,128]{2,1,0:T(8,128)} all-to-all(f32[8,8,128]{2,1,0:T(8,128)} %get-tuple-element.16), channel_id=1, replica_groups=mesh['seq'=64,'group'=8] {'group'}, dimensions={0} | all-to-all | bytes 65536 | tf_op jit(solution)/shard_map/all_to_all | solution.py:433
  71.4 1.9 %sort_part.1 = f32[64,128]{1,0:T(8,128)} custom-call(f32[8,8,128]{2,1,0:T(8,128)} %all_to_all.16.in_ref), custom_call_target="tpu_custom_call" | custom-call | flops 10000000 | bytes 70000 | tf_op jit(solution)/shard_map/sort_part/pallas_call | solution.py:356
  73.3 30.2 %all_to_all.17 = f32[64,1,128]{2,1,0:T(1,128)} all-to-all(f32[64,1,128]{2,1,0:T(1,128)} %bitcast.15), channel_id=1, replica_groups=mesh['seq'=64,'group'=8] {'seq'}, dimensions={0} | all-to-all | bytes 65536 | tf_op jit(solution)/shard_map/all_to_all | solution.py:435
  103.4 1.8 %finish.1 = (f32[1,256]{1,0:T(1,128)}, f32[1,256]{1,0:T(1,128)}) custom-call(f32[64,128]{1,0:T(8,128)} %bitcast.14), custom_call_target="tpu_custom_call" | custom-call | flops 500000 | bytes 40000 | tf_op jit(solution)/shard_map/finish/pallas_call | solution.py:397
  (1 shorter events, 0.0 us)
Async XLA Ops:
  2.6 7.8 %collective-permute-start = (bf16[272,512]{1,0:T(8,128)(2,1)}, bf16[272,512]{1,0:T(8,128)(2,1)S(1)}, u32[]{:S(2)}, u32[]{:S(2)}) collective-permute-start(bf16[272,512]{1,0:T(8,128)(2,1)} %message.1.refs_3_), channel_id=1, source_target_pairs={{0,16},{8,24},{16,32},{24,40},{32,48},{40,56},{48,64},{56,72},{64,... | collective-permute-start | bytes 835592 | tf_op jit(solution)/shard_map/ppermute | solution.py:408
  10.4 8.5 %collective-permute-start.1 = (bf16[272,512]{1,0:T(8,128)(2,1)S(1)}, bf16[272,512]{1,0:T(8,128)(2,1)S(1)}, u32[]{:S(2)}, u32[]{:S(2)}) collective-permute-start(bf16[272,512]{1,0:T(8,128)(2,1)S(1)} %collective-permute-done.refs_4_), channel_id=1, source_target_pairs={{0,16},{8,24},{16,32},{24,40},{32,48},{40,56},{48,64},{56,72},{64,... | collective-permute-start | bytes 835592 | tf_op jit(solution)/shard_map/ppermute | solution.py:408
  18.9 12.8 %collective-permute-start.2 = (bf16[272,512]{1,0:T(8,128)(2,1)S(1)}, bf16[272,512]{1,0:T(8,128)(2,1)S(1)}, u32[]{:S(2)}, u32[]{:S(2)}) collective-permute-start(bf16[272,512]{1,0:T(8,128)(2,1)S(1)} %collective-permute-done.1.refs_5_), channel_id=1, source_target_pairs={{0,16},{8,24},{16,32},{24,40},{32,48},{40,56},{48,64},{56,72},{64,... | collective-permute-start | bytes 835592 | tf_op jit(solution)/shard_map/ppermute | solution.py:408
  23.8 16.8 %collective-permute-start.4 = (bf16[272,512]{1,0:T(8,128)(2,1)S(1)}, bf16[272,512]{1,0:T(8,128)(2,1)S(1)}, u32[]{:S(2)}, u32[]{:S(2)}) collective-permute-start(bf16[272,512]{1,0:T(8,128)(2,1)S(1)} %collective-permute-done.refs_4_), channel_id=1, source_target_pairs={{0,8},{8,0},{16,24},{24,16},{32,40},{40,32},{48,56},{56,48},{64,72... | collective-permute-start | bytes 835592 | tf_op jit(solution)/shard_map/ppermute | solution.py:412
  29.8 10.9 %collective-permute-start.5 = (bf16[272,512]{1,0:T(8,128)(2,1)S(1)}, bf16[272,512]{1,0:T(8,128)(2,1)S(1)}, u32[]{:S(2)}, u32[]{:S(2)}) collective-permute-start(bf16[272,512]{1,0:T(8,128)(2,1)S(1)} %collective-permute-done.1.refs_5_), channel_id=1, source_target_pairs={{0,8},{8,0},{16,24},{24,16},{32,40},{40,32},{48,56},{56,48},{64,72... | collective-permute-start | bytes 835592 | tf_op jit(solution)/shard_map/ppermute | solution.py:412
  31.7 8.9 %collective-permute-start.3 = (bf16[272,512]{1,0:T(8,128)(2,1)S(1)}, bf16[272,512]{1,0:T(8,128)(2,1)S(1)}, u32[]{:S(2)}, u32[]{:S(2)}) collective-permute-start(bf16[272,512]{1,0:T(8,128)(2,1)S(1)} %broadcast_select_fusion), channel_id=1, source_target_pairs={{8,16},{24,32},{40,48},{56,64},{72,80},{88,96},{104,112},{120,128}... | collective-permute-start | bytes 835592 | tf_op jit(solution)/shard_map/ppermute | solution.py:428
  36.9 3.8 %collective-permute-start.6 = (bf16[272,512]{1,0:T(8,128)(2,1)S(1)}, bf16[272,512]{1,0:T(8,128)(2,1)S(1)}, u32[]{:S(2)}, u32[]{:S(2)}) collective-permute-start(bf16[272,512]{1,0:T(8,128)(2,1)S(1)} %collective-permute-done.2.refs_6_), channel_id=1, source_target_pairs={{0,8},{8,0},{16,24},{24,16},{32,40},{40,32},{48,56},{56,48},{64,72... | collective-permute-start | bytes 835592 | tf_op jit(solution)/shard_map/ppermute | solution.py:412
  40.7 1.0 copy-start
  41.7 1.6 %copy-start.2 = (bf16[1,256,4096]{2,1,0:T(8,128)(2,1)S(1)}, bf16[1,256,4096]{2,1,0:T(8,128)(2,1)}, u32[]{:S(2)}) copy-start(bf16[1,256,4096]{2,1,0:T(8,128)(2,1)} %param.8) | copy-start | bytes 6291460
  43.3 0.7 copy-start.3
  51.4 0.7 copy-start.1

commit v2 on v1

v2 whole, which is shorter than its diff:
```python
import math

import jax
import jax.numpy as jnp
from jax import lax
from jax.experimental import pallas as pl
from jax.experimental.pallas import tpu as pltpu
from jax.sharding import PartitionSpec as P

HD = 128
BLK = 128
TOK = 256
KVH = 4
HEADS = 32
PER = HEADS // KVH
HALF = KVH * HD
KEYS = KVH // 2
LIST = 8
LATE = 5
MSG = TOK + HEADS // 2
TRACE = 0.995
LOG_TRACE = math.log(TRACE)
TO_LOG2 = HD ** -0.5 * math.log2(math.e)
LOW = -1e30
F32 = jnp.float32
BF16 = jnp.bfloat16

NT = (((1,), (1,)), ((), ()))
SMEM = pl.BlockSpec(memory_space=pltpu.SMEM)
VMEM = pl.BlockSpec(memory_space=pltpu.VMEM)
ANY = pl.BlockSpec(memory_space=pl.ANY)


def iota(shape, dim):
    return lax.broadcasted_iota(jnp.int32, shape, dim)


def three(x):
    first = x.astype(BF16)
    rest = x - first.astype(F32)
    second = rest.astype(BF16)
    third = (rest - second.astype(F32)).astype(BF16)
    return first, second, third


def message_kernel(kv_ref, dir_ref, out_ref):
    out_ref[0:TOK, :] = kv_ref[:, 0:HALF]
    direction = dir_ref[...]
    head = iota((HEADS, HD), 0)
    zero = jnp.zeros_like(direction)
    spread = jnp.concatenate(
        [jnp.where(head // PER == k, direction, zero) for k in range(KVH)], axis=1
    )
    read = lax.dot_general(
        spread, kv_ref[:, HALF:], NT, preferred_element_type=F32
    ).astype(BF16)
    out_ref[TOK:MSG, 0:TOK] = read[0 : HEADS // 2]
    out_ref[TOK:MSG, TOK:HALF] = read[HEADS // 2 :]


def message(kv, direction):
    return pl.pallas_call(
        message_kernel,
        out_shape=jax.ShapeDtypeStruct((MSG, HALF), BF16),
        in_specs=[VMEM, VMEM],
        out_specs=VMEM,
        cost_estimate=pl.CostEstimate(
            flops=2 * TOK * HALF * HEADS, bytes_accessed=800_000, transcendentals=0
        ),
        name="message",
    )(kv, direction)


def weights(shard, rew_ref, turn_ref, base_ref, dest_ref):
    sub, lane = iota((TOK, TOK), 0), iota((TOK, TOK), 1)
    diag = sub == lane

    def column(row):
        return jnp.sum(jnp.where(diag, row, 0.0), axis=1, keepdims=True)

    spot = iota((1, TOK), 1)
    begins = (turn_ref[...] == 1) | ((shard == 0) & (spot == 0))
    start_row = jnp.where(begins, 1.0, 0.0)
    start_col = column(start_row)
    c_row = jnp.sum(jnp.where(sub <= lane, start_col, 0.0), axis=0, keepdims=True)
    c_col = jnp.sum(jnp.where(lane <= sub, start_row, 0.0), axis=1, keepdims=True)
    rewards = column(rew_ref[...])
    base = column(base_ref[...])
    gap = c_col - c_row
    opens = start_col > 0.5
    m = jnp.where((sub > lane) & opens, (1.0 - TRACE) * jnp.exp((gap - 1.0) * LOG_TRACE), 0.0)
    decay = jnp.where(sub >= lane, jnp.exp(gap * LOG_TRACE), 0.0)
    known = jnp.sum(decay * rewards + m * base, axis=0, keepdims=True)
    total = jnp.sum(start_row, axis=1, keepdims=True)
    b_col = jnp.where(opens, (1.0 - TRACE) * jnp.exp((c_col - 1.0) * LOG_TRACE), 0.0)
    b_row = jnp.sum(jnp.where(diag, b_col, 0.0), axis=0, keepdims=True)
    b_known = jnp.sum(b_col * base + jnp.exp(c_col * LOG_TRACE) * rewards, axis=0, keepdims=True)
    dest = dest_ref[...]
    to_group = lax.rem(dest, 8).astype(F32)
    to_seq = (dest // 8).astype(F32)
    group_col = column(to_group)
    rank = jnp.sum(jnp.where((group_col == to_group) & (lane < sub), 1.0, 0.0), axis=1, keepdims=True)
    slot = (group_col * 32.0 + rank).astype(jnp.int32)
    onehot = jnp.where(slot == lane, 1.0, 0.0).astype(BF16)
    wide = (1, TOK)
    rows = [
        base_ref[...],
        known,
        jnp.exp((total - c_row) * LOG_TRACE),
        to_seq,
        jnp.broadcast_to(jnp.exp(total * LOG_TRACE), wide),
        jnp.broadcast_to(b_known, wide),
        jnp.zeros(wide, F32),
        jnp.zeros(wide, F32),
    ]
    return m, onehot, jnp.concatenate(rows, axis=0), b_row


def attend_kernel(slots, arrays, earlier, place_ref, list_ref, q_ref, *rest):
    count = len(slots)
    has_own = 0 in slots
    msgs, rest = rest[:arrays], rest[arrays:]
    if earlier:
        before_ref, *late_refs = rest[:LATE]
        val_ref, pay_ref, table, score0, score1, found, sems, out_ref = rest[LATE:]
        scores = (score0, score1)
    else:
        out_ref, table, *scores, found, sems = rest
    shard = place_ref[0]
    core = lax.rem(shard, 2)

    copies = []
    sources = [msg.at[at : at + MSG] for msg in msgs for at in range(0, msg.shape[0], MSG)]
    for i, source in enumerate(sources):
        copies.append(pltpu.make_async_copy(source, table.at[i], sems.at[i]))
    for copy in copies:
        copy.start()

    for qb in range(2):
        block = shard * 2 + qb
        n = jnp.int32(0)
        entries = [list_ref[qb, j] for j in range(LIST)]
        for j in range(LIST):
            found[qb, j] = 0
        for j in range(LIST):
            entry = entries[j]
            use = entry < block
            for i in range(j):
                use = use & (entries[i] != entry)
            back = shard - entry // 2
            even = lax.rem(back, 2) == 0
            slot = jnp.where(even, back // 2, 4 + lax.rem(back // 2 + 1 - core, 4))
            local = jnp.int32(0)
            here = jnp.bool_(False)
            for i, s in enumerate(slots):
                hit = slot == s
                local = jnp.where(hit, 2 * i, local)
                here = here | hit
            use = use & here
            at = jnp.minimum(n, LIST - 1)
            found[qb, at] = jnp.where(use, local + lax.rem(entry, 2), found[qb, at])
            n = n + jnp.where(use, 1, 0)
        found[qb, LIST] = n
    out_ref[...] = jnp.zeros_like(out_ref)
    for copy in copies:
        copy.wait()

    causal = iota((BLK, BLK), 1) <= iota((BLK, BLK), 0)
    lane_pair = iota((BLK, 2 * HEADS), 1)
    lane_head = iota((BLK, HEADS), 1)
    ones = jnp.ones((HEADS, BLK), BF16)

    def step(index, carry):
        qb, side = index // 2, lax.rem(index, 2)
        rows = pl.ds(pl.multiple_of(qb * BLK, BLK), BLK)
        n = found[qb, LIST]

        def run(blocks):
            codes = [qb] if has_own else []
            codes += [found[qb, j] for j in range(blocks - len(codes))]
            spots = [(code // 2, pl.multiple_of(lax.rem(code, 2) * BLK, BLK)) for code in codes]
            read = jnp.concatenate(
                [
                    jnp.concatenate(
                        [
                            table[i, TOK:MSG, pl.ds(at, BLK)],
                            table[i, TOK:MSG, pl.ds(pl.multiple_of(at + TOK, BLK), BLK)],
                        ],
                        axis=0,
                    )
                    for i, at in spots
                ],
                axis=1,
            )
            read = jnp.concatenate([read, jnp.concatenate([ones] * blocks, axis=1)], axis=0)
            spare = jnp.where(n + has_own == blocks, 0.0, LOW)
            for k in range(KEYS):
                first = (side * KEYS + k) * PER * HD
                heads = [q_ref[rows, pl.ds(pl.multiple_of(first + g * HD, HD), HD)] for g in range(PER)]
                query = jnp.concatenate(heads, axis=0)
                own = pl.ds(pl.multiple_of((side * KEYS + k) * HD, HD), HD)
                for j in range(0, blocks, 2):
                    both = jnp.concatenate([table[i, pl.ds(at, BLK), own] for i, at in spots[j : j + 2]], axis=0)
                    scores[k][:, j * BLK : (j + 2) * BLK] = lax.dot_general(
                        query, both, NT, preferred_element_type=F32
                    )
            sums = jnp.zeros((BLK, 2 * HEADS), F32)
            peaks = jnp.zeros((BLK, HEADS), F32)
            for k in range(KEYS):
                for g in range(PER):
                    parts = []
                    for j in range(blocks):
                        s = scores[k][g * BLK : (g + 1) * BLK, j * BLK : (j + 1) * BLK]
                        if has_own and j == 0:
                            s = jnp.where(causal, s, LOW)
                        elif j == blocks - 1:
                            s = s + spare
                        parts.append(s)
                    top = parts[0]
                    for s in parts[1:]:
                        top = jnp.maximum(top, s)
                    peak = jnp.max(top, axis=1, keepdims=True) * TO_LOG2
                    p = jnp.concatenate([jnp.exp2(s * TO_LOG2 - peak).astype(BF16) for s in parts], axis=1)
                    both = lax.dot_general(p, read, NT, preferred_element_type=F32)
                    head = (side * KEYS + k) * PER + g
                    sums = jnp.where((lane_pair == head) | (lane_pair == head + HEADS), both, sums)
                    peaks = jnp.where(lane_head == head, peak, peaks)
            out_ref[0, rows, 0 : 2 * HEADS] += sums
            out_ref[1, rows, 0:HEADS] += peaks

        def nothing():
            mine = lane_head // (HEADS // 2) == side
            out_ref[1, rows, 0:HEADS] += jnp.where(mine, LOW, 0.0)

        most = min(LIST, 2 * count) + has_own
        for pairs in range((most + 1) // 2 + 1):
            if pairs == 0 and has_own:
                continue

            @pl.when((n + has_own + 1) // 2 == pairs)
            def _(pairs=pairs):
                if pairs:
                    run(2 * pairs)
                else:
                    nothing()

        return carry

    lax.fori_loop(0, 4, step, 0)

    if earlier:
        every = [out_ref, before_ref]
        peaks = [ref[1, :, 0:HEADS] for ref in every]
        top = peaks[0]
        for peak in peaks[1:]:
            top = jnp.maximum(top, peak)
        total = summed = 0.0
        for ref, peak in zip(every, peaks):
            weight = jnp.exp2(peak - top)
            total = total + ref[0, :, HEADS : 2 * HEADS] * weight
            summed = summed + ref[0, :, 0:HEADS] * weight
        att = jnp.sum(summed / total, axis=1, keepdims=True)
        diag = iota((TOK, TOK), 0) == iota((TOK, TOK), 1)
        m, onehot, fields, b_row = weights(shard, *late_refs)
        att_row = jnp.sum(jnp.where(diag, att, 0.0), axis=0, keepdims=True)
        value = fields[0:1] + att_row
        val_ref[...] = value
        local = fields[1:2] + jnp.sum(m * att, axis=0, keepdims=True)
        b = fields[5:6] + jnp.sum(b_row * att_row, axis=1, keepdims=True)
        lines = jnp.concatenate([value, local, fields[2:5], b, fields[6:8]], axis=0)
        split = jnp.concatenate(three(lines), axis=0)
        moved = jnp.dot(split, onehot, preferred_element_type=F32)
        moved = moved[0:8] + moved[8:16] + moved[16:24]
        pay_ref[...] = jnp.zeros_like(pay_ref)
        for g in range(8):
            pay_ref[g, :, 0:32] = moved[:, g * 32 : (g + 1) * 32]


def attend(slots, place, lists, q, msgs, befores=(), extra=()):
    count = len(slots)
    partial = (2, TOK, BLK)
    most = min(LIST, 2 * count) + 2
    scratch = [
        pltpu.VMEM((count, MSG, HALF), BF16),
        pltpu.VMEM((PER * BLK, most * BLK), F32),
        pltpu.VMEM((PER * BLK, most * BLK), F32),
        pltpu.SMEM((2, LIST + 1), jnp.int32),
        pltpu.SemaphoreType.DMA((count,)),
    ]
    late = ()
    if befores:
        out_shape = (jax.ShapeDtypeStruct((1, TOK), F32), jax.ShapeDtypeStruct((8, 8, HD), F32))
        out_specs = (VMEM, VMEM)
        late = (*befores, *extra)
        scratch.append(pltpu.VMEM(partial, F32))
    else:
        out_shape, out_specs = jax.ShapeDtypeStruct(partial, F32), VMEM
    return pl.pallas_call(
        lambda *refs: attend_kernel(slots, len(msgs), len(befores), *refs),
        out_shape=out_shape,
        in_specs=[SMEM, SMEM, VMEM] + [ANY] * len(msgs) + [VMEM] * len(late),
        out_specs=out_specs,
        scratch_shapes=scratch,
        compiler_params=pltpu.CompilerParams(vmem_limit_bytes=32 * 1024 * 1024),
        cost_estimate=pl.CostEstimate(
            flops=1_000_000, bytes_accessed=100_000, transcendentals=0
        ),
        name="attend",
    )(place, lists, q, *msgs, *late)


def sort_kernel(in_ref, out_ref):
    seqs = iota((64, HD), 0)
    lane = iota((64, HD), 1)
    before = jnp.where(iota((HD, HD), 0) < iota((HD, HD), 1), 1.0, 0.0).astype(BF16)
    ahead = jnp.zeros((64, 1), F32)
    onehots, fields = [], []
    known = jnp.zeros((1, HD), F32)
    lane_row = iota((1, HD), 1)
    zero = jnp.zeros((1, HD), F32)
    for g in range(8):
        x = in_ref[g]
        tag = x[3:4].astype(jnp.int32)
        hit = (seqs == tag) & (lane < 32)
        one = jnp.where(hit, 1.0, 0.0)
        onehot = one.astype(BF16)
        counts = jnp.dot(onehot, before, preferred_element_type=F32) + ahead
        rank = jnp.sum(one * counts, axis=0, keepdims=True)
        ahead = ahead + jnp.sum(one, axis=1, keepdims=True)
        group = jnp.full((1, HD), float(g), F32)
        rows = [
            jnp.where(rank == float(r), f, zero)
            for f in (x[0:1], x[1:2], x[2:3], group)
            for r in range(4)
        ]
        onehots.append(onehot)
        fields.append(jnp.concatenate(rows, axis=0))
        known = jnp.where(lane_row == 16 + g, x[4:5, 0:1], known)
        known = jnp.where(lane_row == 24 + g, x[5:6, 0:1], known)
    table = jnp.concatenate(fields, axis=1)
    table = jnp.concatenate([table, jnp.zeros((HD - 16, 8 * HD), F32)], axis=0)
    onehot = jnp.concatenate(onehots, axis=1)
    moved = 0.0
    for part in three(table):
        moved = moved + lax.dot_general(onehot, part, NT, preferred_element_type=F32)
    out_ref[...] = moved + known


def sort_part(received):
    return pl.pallas_call(
        sort_kernel,
        out_shape=jax.ShapeDtypeStruct((64, HD), F32),
        in_specs=[VMEM],
        out_specs=VMEM,
        cost_estimate=pl.CostEstimate(flops=10_000_000, bytes_accessed=70_000, transcendentals=0),
        name="sort_part",
    )(received)


def finish_kernel(in_ref, adv_ref, ret_ref):
    x = in_ref[...]
    seqs = iota((64, HD), 0)
    lane = iota((64, HD), 1)
    factor = x
    offset = pltpu.roll(x, HD - 8, axis=1)
    span = 1
    while span < 64:
        inside = seqs < 64 - span
        next_factor = jnp.where(inside, pltpu.roll(factor, 64 - span, axis=0), 1.0)
        next_offset = jnp.where(inside, pltpu.roll(offset, 64 - span, axis=0), 0.0)
        offset = offset + factor * next_offset
        factor = factor * next_factor
        span *= 2
    incoming = jnp.where(seqs < 63, pltpu.roll(offset, 63, axis=0), 0.0)
    wide = (64, TOK)
    spot = iota(wide, 1) - 4 * iota(wide, 0)
    adv = jnp.zeros(wide, F32)
    ret = jnp.zeros(wide, F32)
    for r in range(4):
        group = x[:, 12 + r : 13 + r].astype(jnp.int32)
        entry = jnp.sum(jnp.where(lane == group + 16, incoming, 0.0), axis=1, keepdims=True)
        returns = x[:, 4 + r : 5 + r] + x[:, 8 + r : 9 + r] * entry
        advantage = returns - x[:, r : r + 1]
        adv = jnp.where(spot == r, advantage, adv)
        ret = jnp.where(spot == r, returns, ret)
    adv_ref[...] = jnp.sum(adv, axis=0, keepdims=True)
    ret_ref[...] = jnp.sum(ret, axis=0, keepdims=True)


def finish(arrived):
    return pl.pallas_call(
        finish_kernel,
        out_shape=(jax.ShapeDtypeStruct((1, TOK), F32),) * 2,
        in_specs=[VMEM],
        out_specs=(VMEM, VMEM),
        cost_estimate=pl.CostEstimate(flops=500_000, bytes_accessed=40_000, transcendentals=0),
        name="finish",
    )(arrived)


YS = 8


def swap(value, count):
    return lax.ppermute(value, "seq", [(s, s ^ 1) for s in range(count)])


def hop(value, chips, count):
    return lax.ppermute(value, "seq", [(s, s + 2 * chips) for s in range(count - 2 * chips)])


def place_of(x, y, core):
    return (x * YS + y) * 2 + core


def shards(queries, keys_values, block_list, value_dir, base_values, rewards, turn_start, actor_shard):
    count = lax.axis_size("seq")
    shard = lax.axis_index("seq").astype(jnp.int32)
    place = shard[None]
    core = shard % 2
    heads = (place, block_list[0], queries[0])
    own = message(keys_values[0], value_dir.reshape(HEADS, HD))
    a = hop(own, 1, count)
    b = hop(own, 2, count)
    back, last = [], []
    for s in range(count):
        x, y = s // (2 * YS), s // 2 % YS
        if s % 2 == 0:
            last.append((s, s + 1))
        elif s + 7 < count:
            between = place_of(x, (y - 2) % YS, 1)
            back.append((s, between))
            last.append((between, s + 7))
    relayed = lax.ppermute(own, "seq", back)
    sums0 = attend((0, 1), *heads, (own, a))
    sent = jnp.where(core == 0, own, relayed)
    a, b, sent, sums0 = lax.optimization_barrier((a, b, sent, sums0))
    c = hop(b, 1, count)
    far = lax.ppermute(sent, "seq", last)
    wab = swap(jnp.concatenate([a, b], axis=0), count)
    wc = swap(c, count)
    extra = (rewards, turn_start, base_values, actor_shard)
    values, payload = attend((5, 6, 2, 4, 3, 7), *heads, (wab, b, far, c, wc), (sums0,), extra)
    received = lax.all_to_all(payload, "group", split_axis=0, concat_axis=0, tiled=True)
    arranged = sort_part(received)
    arrived = lax.all_to_all(arranged, "seq", split_axis=0, concat_axis=0, tiled=True)
    advantage, returns = finish(arrived)
    return values, advantage.reshape(TOK), returns.reshape(TOK)


def solution(mesh):
    placed = (
        P("group", "seq", None),
        P("group", "seq", None),
        P("group", "seq", None),
        P(),
        P("group", "seq"),
        P("group", "seq"),
        P("group", "seq"),
        P("group", "seq"),
    )
    return jax.shard_map(
        shards,
        mesh=mesh,
        in_specs=placed,
        out_specs=(P("group", "seq"), P(("seq", "group")), P(("seq", "group"))),
        check_vma=False,
    )
```

time: 106 us -> 102 us (0.962)
  waiting for transfers between devices: 7.24 us -> 4.08 us
  blocking collectives: 47.3 us -> 50.2 us
  Pallas kernels: 17.1 us -> 15.1 us
    ppermute x3 -> x2, starting transfers between devices: 9.76 us -> 4.77 us  [swap(): return lax.ppermute(value, 'seq', [(s, s ^ 1) for s in range(count)])]
    ppermute x4 -> x5, starting transfers between devices: 19.1 us -> 23.5 us  [the longest x3 13.3 us: hop(): lax.ppermute(value, 'seq', [(s, s + 2 * chips) for s in range(count - 2 *...]
    all_to_all x1, blocking collectives: 30.2 us -> 33.4 us  [shards(): lax.all_to_all(arranged, 'seq', split_axis=0, concat_axis=0, tiled=True)]
    ppermute x4 -> x5, waiting for transfers between devices: 7.24 us -> 4.07 us  [the longest x1 4.06 us: shards(): far = lax.ppermute(sent, 'seq', last)]
    pallas_call x3 -> x2, Pallas kernels: 11.4 us -> 9.49 us  [attend(): pl.pallas_call(lambda *refs: attend_kernel(slots, len(msgs), len(befores)...]
    unnamed x8 -> x16, local copies, waits for them, and re-layouts: 3.95 us -> 3.25 us
  transfers between devices with their start and end apart: 7 -> 7, of which waited for: 2 -> 1; matrix products, arithmetic and copies ran while one was open for 0% -> 0% of each run, Pallas kernels for 2% -> 5%
where the time goes in v2:
time: 102 us
  blocking collectives  50.2 us (49%)
  starting transfers between devices  28.2 us (28%)
  Pallas kernels  15.1 us (15%)
  waiting for transfers between devices  4.08 us (4%)
  local copies, waits for them, and re-layouts  3.25 us (3%)
    all_to_all x1, blocking collectives, shards(): lax.all_to_all(arranged, 'seq', split_axis=0, concat_axis=0, tiled=True)  33.4 us
    all_to_all x1, blocking collectives, shards(): lax.all_to_all(payload, 'group', split_axis=0, concat_axis=0, tiled=True)  16.8 us
    ppermute x3, starting transfers between devices, hop(): lax.ppermute(value, 'seq', [(s, s + 2 * chips) for s in range(count - 2 *...  13.3 us
    pallas_call x2, Pallas kernels, attend(): pl.pallas_call(lambda *refs: attend_kernel(slots, len(msgs), len(befores)...  9.49 us
    ppermute x1, starting transfers between devices, shards(): far = lax.ppermute(sent, 'seq', last)  5.15 us
    ppermute x1, starting transfers between devices, shards(): relayed = lax.ppermute(own, 'seq', back)  4.97 us
    ppermute x2, starting transfers between devices, swap(): return lax.ppermute(value, 'seq', [(s, s ^ 1) for s in range(count)])  4.77 us
    ppermute x1, waiting for transfers between devices, shards(): far = lax.ppermute(sent, 'seq', last)  4.06 us
  transfers between devices with their start and end apart: 7, of which 1 were waited for; matrix products, arithmetic and copies ran while one was open for 0% of the time, Pallas kernels for 5%

profile of v2, /device:TPU:1, one launch (start us, length us, event | category | flops | bytes accessed | tf_op | source)
XLA Modules:
  0.0 101.8 jit_solution(11928022655102032891)
XLA Ops:
  0.6 1.9 %message.1.refs_3_ = bf16[272,512]{1,0:T(8,128)(2,1)} custom-call(bf16[256,1024]{1,0:T(8,128)(2,1)} %bitcast.15, bf16[32,128]{1,0:T(8,128)(2,1)} %bitcast.18), custom_call_target="tpu_custom_call" | custom-call | flops 8388608 | bytes 800000 | tf_op jit(solution)/shard_map/message/pallas_call | solution.py:62
  2.6 4.0 %collective-permute-start = (bf16[272,512]{1,0:T(8,128)(2,1)}, bf16[272,512]{1,0:T(8,128)(2,1)S(1)}, u32[]{:S(2)}, u32[]{:S(2)}) collective-permute-start(bf16[272,512]{1,0:T(8,128)(2,1)} %message.1.refs_3_), channel_id=1, source_target_pairs={{0,16},{8,24},{16,32},{24,40},{32,48},{40,56},{48,64},{56,72},{64,... | collective-permute-start | bytes 835592 | tf_op jit(solution)/shard_map/ppermute | solution.py:409
  6.6 5.0 %collective-permute-start.2 = (bf16[272,512]{1,0:T(8,128)(2,1)}, bf16[272,512]{1,0:T(8,128)(2,1)S(1)}, u32[]{:S(2)}, u32[]{:S(2)}) collective-permute-start(bf16[272,512]{1,0:T(8,128)(2,1)} %message.1.refs_3_), channel_id=1, source_target_pairs={{8,104},{24,120},{40,8},{56,24},{72,40},{88,56},{104,72},{120,88},... | collective-permute-start | bytes 835592 | tf_op jit(solution)/shard_map/ppermute | solution.py:434
  11.6 1.3 %collective-permute-start.1 = (bf16[272,512]{1,0:T(8,128)(2,1)}, bf16[272,512]{1,0:T(8,128)(2,1)S(1)}, u32[]{:S(2)}, u32[]{:S(2)}) collective-permute-start(bf16[272,512]{1,0:T(8,128)(2,1)} %message.1.refs_3_), channel_id=1, source_target_pairs={{0,32},{8,40},{16,48},{24,56},{32,64},{40,72},{48,80},{56,88},{64,... | collective-permute-start | bytes 835592 | tf_op jit(solution)/shard_map/ppermute | solution.py:409
  12.9 0.0 collective-permute-done.refs_4_
  12.9 0.0 copy-start
  12.9 1.6 %copy-done = bf16[1,256,4096]{2,1,0:T(8,128)(2,1)S(1)} copy-done((bf16[1,256,4096]{2,1,0:T(8,128)(2,1)S(1)}, bf16[1,256,4096]{2,1,0:T(8,128)(2,1)}, u32[]{:S(2)}) %copy-start) | copy-done | bytes 2097176
  14.5 1.0 copy-done.2
  15.5 0.7 copy-done.3
  16.2 5.0 %attend.2.refs_8_ = f32[2,256,128]{2,1,0:T(8,128)S(1)} custom-call(s32[1]{0:T(128)} %bitcast.refs_0_, s32[2,8]{1,0:T(2,128)S(1)} %bitcast.13, bf16[256,4096]{1,0:T(8,128)(2,1)S(1)} %bitcast.11, bf16[272,512]{1,0:T(8,128)(2,1)S(1)} %copy-done.2, bf16[272,512]{1,0:T(8,128)(2,1)S(1)} %collective-permute-done.refs_4_), custom_call_target="tpu_custom_call" | custom-call | flops 1000000 | bytes 100000 | tf_op jit(solution)/shard_map/attend/pallas_call | solution.py:298
  21.1 0.0 copy-start.4
  21.2 0.0 copy-start.5
  21.2 0.0 copy-start.6
  21.2 0.0 copy-start.7
  21.2 0.0 collective-permute-done.2
  21.2 0.0 collective-permute-done.1.refs_4_
  21.3 8.0 %collective-permute-start.5 = (bf16[272,512]{1,0:T(8,128)(2,1)S(1)}, bf16[272,512]{1,0:T(8,128)(2,1)S(1)}, u32[]{:S(2)}, u32[]{:S(2)}) collective-permute-start(bf16[272,512]{1,0:T(8,128)(2,1)S(1)} %collective-permute-done.1.refs_4_), channel_id=1, source_target_pairs={{0,16},{8,24},{16,32},{24,40},{32,48},{40,56},{48,64},{56,72},{64,... | collective-permute-start | bytes 835592 | tf_op jit(solution)/shard_map/ppermute | solution.py:409
  29.3 2.7 %collective-permute-start.3 = (bf16[544,512]{1,0:T(8,128)(2,1)S(1)}, bf16[544,512]{1,0:T(8,128)(2,1)S(1)}, u32[]{:S(2)}, u32[]{:S(2)}) collective-permute-start(bf16[544,512]{1,0:T(8,128)(2,1)S(1)} %pad_maximum_fusion), channel_id=1, source_target_pairs={{0,8},{8,0},{16,24},{24,16},{32,40},{40,32},{48,56},{56,48},{64,72... | collective-permute-start | bytes 1671176 | tf_op jit(solution)/shard_map/ppermute | solution.py:405
  32.0 5.1 %collective-permute-start.4 = (bf16[272,512]{1,0:T(8,128)(2,1)S(1)}, bf16[272,512]{1,0:T(8,128)(2,1)S(1)}, u32[]{:S(2)}, u32[]{:S(2)}) collective-permute-start(bf16[272,512]{1,0:T(8,128)(2,1)S(1)} %broadcast_select_fusion), channel_id=1, source_target_pairs={{0,8},{104,64},{16,24},{120,80},{32,40},{8,96},{48,56},{24,112},{6... | collective-permute-start | bytes 835592 | tf_op jit(solution)/shard_map/ppermute | solution.py:439
  37.1 0.0 collective-permute-done.5.refs_6_
  37.1 2.1 %collective-permute-start.6 = (bf16[272,512]{1,0:T(8,128)(2,1)S(1)}, bf16[272,512]{1,0:T(8,128)(2,1)S(1)}, u32[]{:S(2)}, u32[]{:S(2)}) collective-permute-start(bf16[272,512]{1,0:T(8,128)(2,1)S(1)} %collective-permute-done.5.refs_6_), channel_id=1, source_target_pairs={{0,8},{8,0},{16,24},{24,16},{32,40},{40,32},{48,56},{56,48},{64,72... | collective-permute-start | bytes 835592 | tf_op jit(solution)/shard_map/ppermute | solution.py:405
  39.3 4.1 %collective-permute-done.4.refs_5_ = bf16[272,512]{1,0:T(8,128)(2,1)S(1)} collective-permute-done((bf16[272,512]{1,0:T(8,128)(2,1)S(1)}, bf16[272,512]{1,0:T(8,128)(2,1)S(1)}, u32[]{:S(2)}, u32[]{:S(2)}) %collective-permute-start.4) | collective-permute-done | bytes 278560 | tf_op jit(solution)/shard_map/ppermute | solution.py:439
  43.3 0.0 collective-permute-done.3.refs_3_
  43.3 0.0 collective-permute-done.6.refs_7_
  43.3 0.0 copy-done.4
  43.3 0.0 copy-done.5
  43.4 0.0 copy-done.6
  43.4 4.5 %attend.3 = (f32[1,256]{1,0:T(1,128)}, f32[8,8,128]{2,1,0:T(8,128)S(1)}) custom-call(s32[1]{0:T(128)} %bitcast.refs_0_, s32[2,8]{1,0:T(2,128)S(1)} %bitcast.14, bf16[256,4096]{1,0:T(8,128)(2,1)S(1)} %bitcast.12, bf16[544,512]{1,0:T(8,128)(2,1)S(1)} %collective-permute-done.3.refs_3_, bf16[272,512]{1,0:T(8,128)(2,1)S(1)} %collective-permute-done.1.refs_4_, ...), custom_call_target="tpu_custom_call" | custom-call | flops 1000000 | bytes 100000 | tf_op jit(solution)/shard_map/attend/pallas_call | solution.py:298
  47.9 16.8 %all_to_all.16.in_ref = f32[8,8,128]{2,1,0:T(8,128)} all-to-all(f32[8,8,128]{2,1,0:T(8,128)S(1)} %get-tuple-element.16), channel_id=1, replica_groups=mesh['seq'=64,'group'=8] {'group'}, dimensions={0} | all-to-all | bytes 65536 | tf_op jit(solution)/shard_map/all_to_all | solution.py:444
  64.7 1.9 %sort_part.1 = f32[64,128]{1,0:T(8,128)} custom-call(f32[8,8,128]{2,1,0:T(8,128)} %all_to_all.16.in_ref), custom_call_target="tpu_custom_call" | custom-call | flops 10000000 | bytes 70000 | tf_op jit(solution)/shard_map/sort_part/pallas_call | solution.py:350
  66.6 33.4 %all_to_all.17 = f32[64,1,128]{2,1,0:T(1,128)} all-to-all(f32[64,1,128]{2,1,0:T(1,128)} %bitcast.17), channel_id=1, replica_groups=mesh['seq'=64,'group'=8] {'seq'}, dimensions={0} | all-to-all | bytes 65536 | tf_op jit(solution)/shard_map/all_to_all | solution.py:446
  100.0 1.8 %finish.1 = (f32[1,256]{1,0:T(1,128)}, f32[1,256]{1,0:T(1,128)}) custom-call(f32[64,128]{1,0:T(8,128)} %bitcast.16), custom_call_target="tpu_custom_call" | custom-call | flops 500000 | bytes 40000 | tf_op jit(solution)/shard_map/finish/pallas_call | solution.py:391
  (7 shorter events, 0.1 us)
Async XLA Ops:
  2.6 10.4 %collective-permute-start = (bf16[272,512]{1,0:T(8,128)(2,1)}, bf16[272,512]{1,0:T(8,128)(2,1)S(1)}, u32[]{:S(2)}, u32[]{:S(2)}) collective-permute-start(bf16[272,512]{1,0:T(8,128)(2,1)} %message.1.refs_3_), channel_id=1, source_target_pairs={{0,16},{8,24},{16,32},{24,40},{32,48},{40,56},{48,64},{56,72},{64,... | collective-permute-start | bytes 835592 | tf_op jit(solution)/shard_map/ppermute | solution.py:409
  6.6 14.6 %collective-permute-start.2 = (bf16[272,512]{1,0:T(8,128)(2,1)}, bf16[272,512]{1,0:T(8,128)(2,1)S(1)}, u32[]{:S(2)}, u32[]{:S(2)}) collective-permute-start(bf16[272,512]{1,0:T(8,128)(2,1)} %message.1.refs_3_), channel_id=1, source_target_pairs={{8,104},{24,120},{40,8},{56,24},{72,40},{88,56},{104,72},{120,88},... | collective-permute-start | bytes 835592 | tf_op jit(solution)/shard_map/ppermute | solution.py:434
  11.6 9.7 %collective-permute-start.1 = (bf16[272,512]{1,0:T(8,128)(2,1)}, bf16[272,512]{1,0:T(8,128)(2,1)S(1)}, u32[]{:S(2)}, u32[]{:S(2)}) collective-permute-start(bf16[272,512]{1,0:T(8,128)(2,1)} %message.1.refs_3_), channel_id=1, source_target_pairs={{0,32},{8,40},{16,48},{24,56},{32,64},{40,72},{48,80},{56,88},{64,... | collective-permute-start | bytes 835592 | tf_op jit(solution)/shard_map/ppermute | solution.py:409
  12.9 1.6 %copy-start = (bf16[1,256,4096]{2,1,0:T(8,128)(2,1)S(1)}, bf16[1,256,4096]{2,1,0:T(8,128)(2,1)}, u32[]{:S(2)}) copy-start(bf16[1,256,4096]{2,1,0:T(8,128)(2,1)} %param.8) | copy-start | bytes 6291460
  14.5 1.0 copy-start.2
  15.5 0.7 copy-start.3
  16.1 27.2 %copy-start.1 = (bf16[1,256,4096]{2,1,0:T(8,128)(2,1)S(1)}, bf16[1,256,4096]{2,1,0:T(8,128)(2,1)}, u32[]{:S(2)}) copy-start(bf16[1,256,4096]{2,1,0:T(8,128)(2,1)} %param.8) | copy-start | bytes 6291460
  21.1 22.2 %copy-start.4 = (f32[1,256]{1,0:T(1,128)S(1)}, f32[1,256]{1,0:T(1,128)}, u32[]{:S(2)}) copy-start(f32[1,256]{1,0:T(1,128)} %refs_9_.1) | copy-start | bytes 3076
  21.2 22.2 %copy-start.5 = (s32[1,256]{1,0:T(1,128)S(1)}, s32[1,256]{1,0:T(1,128)}, u32[]{:S(2)}) copy-start(s32[1,256]{1,0:T(1,128)} %refs_10_.1) | copy-start | bytes 3076
  21.2 22.2 %copy-start.6 = (f32[1,256]{1,0:T(1,128)S(1)}, f32[1,256]{1,0:T(1,128)}, u32[]{:S(2)}) copy-start(f32[1,256]{1,0:T(1,128)} %refs_11_.1) | copy-start | bytes 3076
  21.2 22.2 %copy-start.7 = (s32[1,256]{1,0:T(1,128)S(1)}, s32[1,256]{1,0:T(1,128)}, u32[]{:S(2)}) copy-start(s32[1,256]{1,0:T(1,128)} %refs_12_.1) | copy-start | bytes 3076
  21.3 15.9 %collective-permute-start.5 = (bf16[272,512]{1,0:T(8,128)(2,1)S(1)}, bf16[272,512]{1,0:T(8,128)(2,1)S(1)}, u32[]{:S(2)}, u32[]{:S(2)}) collective-permute-start(bf16[272,512]{1,0:T(8,128)(2,1)S(1)} %collective-permute-done.1.refs_4_), channel_id=1, source_target_pairs={{0,16},{8,24},{16,32},{24,40},{32,48},{40,56},{48,64},{56,72},{64,... | collective-permute-start | bytes 835592 | tf_op jit(solution)/shard_map/ppermute | solution.py:409
  29.3 14.0 %collective-permute-start.3 = (bf16[544,512]{1,0:T(8,128)(2,1)S(1)}, bf16[544,512]{1,0:T(8,128)(2,1)S(1)}, u32[]{:S(2)}, u32[]{:S(2)}) collective-permute-start(bf16[544,512]{1,0:T(8,128)(2,1)S(1)} %pad_maximum_fusion), channel_id=1, source_target_pairs={{0,8},{8,0},{16,24},{24,16},{32,40},{40,32},{48,56},{56,48},{64,72... | collective-permute-start | bytes 1671176 | tf_op jit(solution)/shard_map/ppermute | solution.py:405
  32.0 11.3 %collective-permute-start.4 = (bf16[272,512]{1,0:T(8,128)(2,1)S(1)}, bf16[272,512]{1,0:T(8,128)(2,1)S(1)}, u32[]{:S(2)}, u32[]{:S(2)}) collective-permute-start(bf16[272,512]{1,0:T(8,128)(2,1)S(1)} %broadcast_select_fusion), channel_id=1, source_target_pairs={{0,8},{104,64},{16,24},{120,80},{32,40},{8,96},{48,56},{24,112},{6... | collective-permute-start | bytes 835592 | tf_op jit(solution)/shard_map/ppermute | solution.py:439
  37.1 6.2 %collective-permute-start.6 = (bf16[272,512]{1,0:T(8,128)(2,1)S(1)}, bf16[272,512]{1,0:T(8,128)(2,1)S(1)}, u32[]{:S(2)}, u32[]{:S(2)}) collective-permute-start(bf16[272,512]{1,0:T(8,128)(2,1)S(1)} %collective-permute-done.5.refs_6_), channel_id=1, source_target_pairs={{0,8},{8,0},{16,24},{24,16},{32,40},{40,32},{48,56},{56,48},{64,72... | collective-permute-start | bytes 835592 | tf_op jit(solution)/shard_map/ppermute | solution.py:405

commit v3 on v2

--- a/solution.py
+++ b/solution.py
@@ -162,6 +162,8 @@
             n = n + jnp.where(use, 1, 0)
         found[qb, LIST] = n
     out_ref[...] = jnp.zeros_like(out_ref)
+    if earlier:
+        m, onehot, fields, b_row = weights(shard, *late_refs)
     for copy in copies:
         copy.wait()
 
@@ -193,7 +195,6 @@
                 axis=1,
             )
             read = jnp.concatenate([read, jnp.concatenate([ones] * blocks, axis=1)], axis=0)
-            spare = jnp.where(n + has_own == blocks, 0.0, LOW)
             for k in range(KEYS):
                 first = (side * KEYS + k) * PER * HD
                 heads = [q_ref[rows, pl.ds(pl.multiple_of(first + g * HD, HD), HD)] for g in range(PER)]
@@ -201,7 +202,7 @@
                 own = pl.ds(pl.multiple_of((side * KEYS + k) * HD, HD), HD)
                 for j in range(0, blocks, 2):
                     both = jnp.concatenate([table[i, pl.ds(at, BLK), own] for i, at in spots[j : j + 2]], axis=0)
-                    scores[k][:, j * BLK : (j + 2) * BLK] = lax.dot_general(
+                    scores[k][:, j * BLK : min(j + 2, blocks) * BLK] = lax.dot_general(
                         query, both, NT, preferred_element_type=F32
                     )
             sums = jnp.zeros((BLK, 2 * HEADS), F32)
@@ -213,8 +214,6 @@
                         s = scores[k][g * BLK : (g + 1) * BLK, j * BLK : (j + 1) * BLK]
                         if has_own and j == 0:
                             s = jnp.where(causal, s, LOW)
-                        elif j == blocks - 1:
-                            s = s + spare
                         parts.append(s)
                     top = parts[0]
                     for s in parts[1:]:
@@ -232,15 +231,12 @@
             mine = lane_head // (HEADS // 2) == side
             out_ref[1, rows, 0:HEADS] += jnp.where(mine, LOW, 0.0)
 
-        most = min(LIST, 2 * count) + has_own
-        for pairs in range((most + 1) // 2 + 1):
-            if pairs == 0 and has_own:
-                continue
-
-            @pl.when((n + has_own + 1) // 2 == pairs)
-            def _(pairs=pairs):
-                if pairs:
-                    run(2 * pairs)
+        for others in range(min(LIST, 2 * count) + 1):
+
+            @pl.when(n == others)
+            def _(others=others):
+                if others + has_own:
+                    run(others + has_own)
                 else:
                     nothing()
 
@@ -261,7 +257,6 @@
             summed = summed + ref[0, :, 0:HEADS] * weight
         att = jnp.sum(summed / total, axis=1, keepdims=True)
         diag = iota((TOK, TOK), 0) == iota((TOK, TOK), 1)
-        m, onehot, fields, b_row = weights(shard, *late_refs)
         att_row = jnp.sum(jnp.where(diag, att, 0.0), axis=0, keepdims=True)
         value = fields[0:1] + att_row
         val_ref[...] = value
@@ -279,7 +274,7 @@
 def attend(slots, place, lists, q, msgs, befores=(), extra=()):
     count = len(slots)
     partial = (2, TOK, BLK)
-    most = min(LIST, 2 * count) + 2
+    most = min(LIST, 2 * count) + (0 in slots)
     scratch = [
         pltpu.VMEM((count, MSG, HALF), BF16),
         pltpu.VMEM((PER * BLK, most * BLK), F32),

time: 102 us -> 101 us (level)
  blocking collectives: 50.2 us -> 46.8 us
  waiting for transfers between devices: 4.08 us -> 5.12 us
    all_to_all x1, blocking collectives: 33.4 us -> 31.5 us  [shards(): lax.all_to_all(arranged, 'seq', split_axis=0, concat_axis=0, tiled=True)]
    all_to_all x1, blocking collectives: 16.8 us -> 15.3 us  [shards(): lax.all_to_all(payload, 'group', split_axis=0, concat_axis=0, tiled=True)]
  transfers between devices with their start and end apart: 7 -> 7, of which waited for: 1 -> 2; matrix products, arithmetic and copies ran while one was open for 0% -> 0% of each run, Pallas kernels for 5% -> 4%
where the time goes in v3:
time: 101 us; the launch traced here: 99.9 us
  blocking collectives  46.8 us (46%)
  starting transfers between devices  28.2 us (28%)
  Pallas kernels  15.5 us (15%)
  waiting for transfers between devices  5.12 us (5%)
  local copies, waits for them, and re-layouts  3.25 us (3%)
    all_to_all x1, blocking collectives, shards(): lax.all_to_all(arranged, 'seq', split_axis=0, concat_axis=0, tiled=True)  31.5 us
    all_to_all x1, blocking collectives, shards(): lax.all_to_all(payload, 'group', split_axis=0, concat_axis=0, tiled=True)  15.3 us
    ppermute x3, starting transfers between devices, hop(): lax.ppermute(value, 'seq', [(s, s + 2 * chips) for s in range(count - 2 *...  13.5 us
    pallas_call x2, Pallas kernels, attend(): pl.pallas_call(lambda *refs: attend_kernel(slots, len(msgs), len(befores)...  9.89 us
    ppermute x1, starting transfers between devices, shards(): far = lax.ppermute(sent, 'seq', last)  5.15 us
    ppermute x1, starting transfers between devices, shards(): relayed = lax.ppermute(own, 'seq', back)  4.97 us
    ppermute x2, starting transfers between devices, swap(): return lax.ppermute(value, 'seq', [(s, s ^ 1) for s in range(count)])  4.59 us
    ppermute x1, waiting for transfers between devices, shards(): far = lax.ppermute(sent, 'seq', last)  4.24 us
  transfers between devices with their start and end apart: 7, of which 2 were waited for; matrix products, arithmetic and copies ran while one was open for 0% of the time, Pallas kernels for 4%

profile of v3, /device:TPU:1, one launch (start us, length us, event | category | flops | bytes accessed | tf_op | source)
XLA Modules:
  0.0 99.9 jit_solution(14922113627800396580)
XLA Ops:
  0.6 1.9 %message.1.refs_3_ = bf16[272,512]{1,0:T(8,128)(2,1)} custom-call(bf16[256,1024]{1,0:T(8,128)(2,1)} %bitcast.15, bf16[32,128]{1,0:T(8,128)(2,1)} %bitcast.18), custom_call_target="tpu_custom_call" | custom-call | flops 8388608 | bytes 800000 | tf_op jit(solution)/shard_map/message/pallas_call | solution.py:62
  2.6 4.0 %collective-permute-start = (bf16[272,512]{1,0:T(8,128)(2,1)}, bf16[272,512]{1,0:T(8,128)(2,1)S(1)}, u32[]{:S(2)}, u32[]{:S(2)}) collective-permute-start(bf16[272,512]{1,0:T(8,128)(2,1)} %message.1.refs_3_), channel_id=1, source_target_pairs={{0,16},{8,24},{16,32},{24,40},{32,48},{40,56},{48,64},{56,72},{64,... | collective-permute-start | bytes 835592 | tf_op jit(solution)/shard_map/ppermute | solution.py:404
  6.6 5.0 %collective-permute-start.2 = (bf16[272,512]{1,0:T(8,128)(2,1)}, bf16[272,512]{1,0:T(8,128)(2,1)S(1)}, u32[]{:S(2)}, u32[]{:S(2)}) collective-permute-start(bf16[272,512]{1,0:T(8,128)(2,1)} %message.1.refs_3_), channel_id=1, source_target_pairs={{8,104},{24,120},{40,8},{56,24},{72,40},{88,56},{104,72},{120,88},... | collective-permute-start | bytes 835592 | tf_op jit(solution)/shard_map/ppermute | solution.py:429
  11.6 1.3 %collective-permute-start.1 = (bf16[272,512]{1,0:T(8,128)(2,1)}, bf16[272,512]{1,0:T(8,128)(2,1)S(1)}, u32[]{:S(2)}, u32[]{:S(2)}) collective-permute-start(bf16[272,512]{1,0:T(8,128)(2,1)} %message.1.refs_3_), channel_id=1, source_target_pairs={{0,32},{8,40},{16,48},{24,56},{32,64},{40,72},{48,80},{56,88},{64,... | collective-permute-start | bytes 835592 | tf_op jit(solution)/shard_map/ppermute | solution.py:404
  12.9 0.0 collective-permute-done.refs_4_
  12.9 0.0 copy-start
  12.9 1.6 %copy-done = bf16[1,256,4096]{2,1,0:T(8,128)(2,1)S(1)} copy-done((bf16[1,256,4096]{2,1,0:T(8,128)(2,1)S(1)}, bf16[1,256,4096]{2,1,0:T(8,128)(2,1)}, u32[]{:S(2)}) %copy-start) | copy-done | bytes 2097176
  14.5 1.0 copy-done.2
  15.5 0.7 copy-done.3
  16.2 3.9 %attend.2.refs_8_ = f32[2,256,128]{2,1,0:T(8,128)S(1)} custom-call(s32[1]{0:T(128)} %bitcast.refs_0_, s32[2,8]{1,0:T(2,128)S(1)} %bitcast.13, bf16[256,4096]{1,0:T(8,128)(2,1)S(1)} %bitcast.11, bf16[272,512]{1,0:T(8,128)(2,1)S(1)} %copy-done.2, bf16[272,512]{1,0:T(8,128)(2,1)S(1)} %collective-permute-done.refs_4_), custom_call_target="tpu_custom_call" | custom-call | flops 1000000 | bytes 100000 | tf_op jit(solution)/shard_map/attend/pallas_call | solution.py:293
  20.1 0.0 copy-start.4
  20.1 0.0 copy-start.5
  20.1 0.0 copy-start.6
  20.1 0.0 copy-start.7
  20.1 0.0 collective-permute-done.2
  20.2 0.9 collective-permute-done.1.refs_4_
  21.1 8.2 %collective-permute-start.5 = (bf16[272,512]{1,0:T(8,128)(2,1)S(1)}, bf16[272,512]{1,0:T(8,128)(2,1)S(1)}, u32[]{:S(2)}, u32[]{:S(2)}) collective-permute-start(bf16[272,512]{1,0:T(8,128)(2,1)S(1)} %collective-permute-done.1.refs_4_), channel_id=1, source_target_pairs={{0,16},{8,24},{16,32},{24,40},{32,48},{40,56},{48,64},{56,72},{64,... | collective-permute-start | bytes 835592 | tf_op jit(solution)/shard_map/ppermute | solution.py:404
  29.3 2.7 %collective-permute-start.3 = (bf16[544,512]{1,0:T(8,128)(2,1)S(1)}, bf16[544,512]{1,0:T(8,128)(2,1)S(1)}, u32[]{:S(2)}, u32[]{:S(2)}) collective-permute-start(bf16[544,512]{1,0:T(8,128)(2,1)S(1)} %pad_maximum_fusion), channel_id=1, source_target_pairs={{0,8},{8,0},{16,24},{24,16},{32,40},{40,32},{48,56},{56,48},{64,72... | collective-permute-start | bytes 1671176 | tf_op jit(solution)/shard_map/ppermute | solution.py:400
  32.0 5.1 %collective-permute-start.4 = (bf16[272,512]{1,0:T(8,128)(2,1)S(1)}, bf16[272,512]{1,0:T(8,128)(2,1)S(1)}, u32[]{:S(2)}, u32[]{:S(2)}) collective-permute-start(bf16[272,512]{1,0:T(8,128)(2,1)S(1)} %broadcast_select_fusion), channel_id=1, source_target_pairs={{0,8},{104,64},{16,24},{120,80},{32,40},{8,96},{48,56},{24,112},{6... | collective-permute-start | bytes 835592 | tf_op jit(solution)/shard_map/ppermute | solution.py:434
  37.1 0.0 collective-permute-done.5.refs_6_
  37.1 1.9 %collective-permute-start.6 = (bf16[272,512]{1,0:T(8,128)(2,1)S(1)}, bf16[272,512]{1,0:T(8,128)(2,1)S(1)}, u32[]{:S(2)}, u32[]{:S(2)}) collective-permute-start(bf16[272,512]{1,0:T(8,128)(2,1)S(1)} %collective-permute-done.5.refs_6_), channel_id=1, source_target_pairs={{0,8},{8,0},{16,24},{24,16},{32,40},{40,32},{48,56},{56,48},{64,72... | collective-permute-start | bytes 835592 | tf_op jit(solution)/shard_map/ppermute | solution.py:400
  39.1 4.2 %collective-permute-done.4.refs_5_ = bf16[272,512]{1,0:T(8,128)(2,1)S(1)} collective-permute-done((bf16[272,512]{1,0:T(8,128)(2,1)S(1)}, bf16[272,512]{1,0:T(8,128)(2,1)S(1)}, u32[]{:S(2)}, u32[]{:S(2)}) %collective-permute-start.4) | collective-permute-done | bytes 278560 | tf_op jit(solution)/shard_map/ppermute | solution.py:434
  43.3 0.0 collective-permute-done.3.refs_3_
  43.3 0.0 collective-permute-done.6.refs_7_
  43.3 0.0 copy-done.1
  43.3 0.0 copy-done.4
  43.3 0.0 copy-done.5
  43.4 5.9 %attend.3 = (f32[1,256]{1,0:T(1,128)}, f32[8,8,128]{2,1,0:T(8,128)S(1)}) custom-call(s32[1]{0:T(128)} %bitcast.refs_0_, s32[2,8]{1,0:T(2,128)S(1)} %bitcast.14, bf16[256,4096]{1,0:T(8,128)(2,1)S(1)} %bitcast.12, bf16[544,512]{1,0:T(8,128)(2,1)S(1)} %collective-permute-done.3.refs_3_, bf16[272,512]{1,0:T(8,128)(2,1)S(1)} %collective-permute-done.1.refs_4_, ...), custom_call_target="tpu_custom_call" | custom-call | flops 1000000 | bytes 100000 | tf_op jit(solution)/shard_map/attend/pallas_call | solution.py:293
  49.3 15.3 %all_to_all.16.in_ref = f32[8,8,128]{2,1,0:T(8,128)} all-to-all(f32[8,8,128]{2,1,0:T(8,128)S(1)} %get-tuple-element.16), channel_id=1, replica_groups=mesh['seq'=64,'group'=8] {'group'}, dimensions={0} | all-to-all | bytes 65536 | tf_op jit(solution)/shard_map/all_to_all | solution.py:439
  64.7 1.9 %sort_part.1 = f32[64,128]{1,0:T(8,128)} custom-call(f32[8,8,128]{2,1,0:T(8,128)} %all_to_all.16.in_ref), custom_call_target="tpu_custom_call" | custom-call | flops 10000000 | bytes 70000 | tf_op jit(solution)/shard_map/sort_part/pallas_call | solution.py:345
  66.5 31.5 %all_to_all.17 = f32[64,1,128]{2,1,0:T(1,128)} all-to-all(f32[64,1,128]{2,1,0:T(1,128)} %bitcast.17), channel_id=1, replica_groups=mesh['seq'=64,'group'=8] {'seq'}, dimensions={0} | all-to-all | bytes 65536 | tf_op jit(solution)/shard_map/all_to_all | solution.py:441
  98.1 1.8 %finish.1 = (f32[1,256]{1,0:T(1,128)}, f32[1,256]{1,0:T(1,128)}) custom-call(f32[64,128]{1,0:T(8,128)} %bitcast.16), custom_call_target="tpu_custom_call" | custom-call | flops 500000 | bytes 40000 | tf_op jit(solution)/shard_map/finish/pallas_call | solution.py:386
  (7 shorter events, 0.1 us)
Async XLA Ops:
  2.6 10.4 %collective-permute-start = (bf16[272,512]{1,0:T(8,128)(2,1)}, bf16[272,512]{1,0:T(8,128)(2,1)S(1)}, u32[]{:S(2)}, u32[]{:S(2)}) collective-permute-start(bf16[272,512]{1,0:T(8,128)(2,1)} %message.1.refs_3_), channel_id=1, source_target_pairs={{0,16},{8,24},{16,32},{24,40},{32,48},{40,56},{48,64},{56,72},{64,... | collective-permute-start | bytes 835592 | tf_op jit(solution)/shard_map/ppermute | solution.py:404
  6.6 13.5 %collective-permute-start.2 = (bf16[272,512]{1,0:T(8,128)(2,1)}, bf16[272,512]{1,0:T(8,128)(2,1)S(1)}, u32[]{:S(2)}, u32[]{:S(2)}) collective-permute-start(bf16[272,512]{1,0:T(8,128)(2,1)} %message.1.refs_3_), channel_id=1, source_target_pairs={{8,104},{24,120},{40,8},{56,24},{72,40},{88,56},{104,72},{120,88},... | collective-permute-start | bytes 835592 | tf_op jit(solution)/shard_map/ppermute | solution.py:429
  11.6 9.5 %collective-permute-start.1 = (bf16[272,512]{1,0:T(8,128)(2,1)}, bf16[272,512]{1,0:T(8,128)(2,1)S(1)}, u32[]{:S(2)}, u32[]{:S(2)}) collective-permute-start(bf16[272,512]{1,0:T(8,128)(2,1)} %message.1.refs_3_), channel_id=1, source_target_pairs={{0,32},{8,40},{16,48},{24,56},{32,64},{40,72},{48,80},{56,88},{64,... | collective-permute-start | bytes 835592 | tf_op jit(solution)/shard_map/ppermute | solution.py:404
  12.9 1.6 %copy-start = (bf16[1,256,4096]{2,1,0:T(8,128)(2,1)S(1)}, bf16[1,256,4096]{2,1,0:T(8,128)(2,1)}, u32[]{:S(2)}) copy-start(bf16[1,256,4096]{2,1,0:T(8,128)(2,1)} %param.8) | copy-start | bytes 6291460
  14.5 1.0 copy-start.2
  15.5 0.7 copy-start.3
  16.1 27.2 %copy-start.1 = (bf16[1,256,4096]{2,1,0:T(8,128)(2,1)S(1)}, bf16[1,256,4096]{2,1,0:T(8,128)(2,1)}, u32[]{:S(2)}) copy-start(bf16[1,256,4096]{2,1,0:T(8,128)(2,1)} %param.8) | copy-start | bytes 6291460
  20.1 23.2 %copy-start.4 = (f32[1,256]{1,0:T(1,128)S(1)}, f32[1,256]{1,0:T(1,128)}, u32[]{:S(2)}) copy-start(f32[1,256]{1,0:T(1,128)} %refs_9_.1) | copy-start | bytes 3076
  20.1 23.2 %copy-start.5 = (s32[1,256]{1,0:T(1,128)S(1)}, s32[1,256]{1,0:T(1,128)}, u32[]{:S(2)}) copy-start(s32[1,256]{1,0:T(1,128)} %refs_10_.1) | copy-start | bytes 3076
  20.1 23.2 %copy-start.6 = (f32[1,256]{1,0:T(1,128)S(1)}, f32[1,256]{1,0:T(1,128)}, u32[]{:S(2)}) copy-start(f32[1,256]{1,0:T(1,128)} %refs_11_.1) | copy-start | bytes 3076
  20.1 23.2 %copy-start.7 = (s32[1,256]{1,0:T(1,128)S(1)}, s32[1,256]{1,0:T(1,128)}, u32[]{:S(2)}) copy-start(s32[1,256]{1,0:T(1,128)} %refs_12_.1) | copy-start | bytes 3076
  21.1 16.1 %collective-permute-start.5 = (bf16[272,512]{1,0:T(8,128)(2,1)S(1)}, bf16[272,512]{1,0:T(8,128)(2,1)S(1)}, u32[]{:S(2)}, u32[]{:S(2)}) collective-permute-start(bf16[272,512]{1,0:T(8,128)(2,1)S(1)} %collective-permute-done.1.refs_4_), channel_id=1, source_target_pairs={{0,16},{8,24},{16,32},{24,40},{32,48},{40,56},{48,64},{56,72},{64,... | collective-permute-start | bytes 835592 | tf_op jit(solution)/shard_map/ppermute | solution.py:404
  29.3 14.0 %collective-permute-start.3 = (bf16[544,512]{1,0:T(8,128)(2,1)S(1)}, bf16[544,512]{1,0:T(8,128)(2,1)S(1)}, u32[]{:S(2)}, u32[]{:S(2)}) collective-permute-start(bf16[544,512]{1,0:T(8,128)(2,1)S(1)} %pad_maximum_fusion), channel_id=1, source_target_pairs={{0,8},{8,0},{16,24},{24,16},{32,40},{40,32},{48,56},{56,48},{64,72... | collective-permute-start | bytes 1671176 | tf_op jit(solution)/shard_map/ppermute | solution.py:400
  32.0 11.3 %collective-permute-start.4 = (bf16[272,512]{1,0:T(8,128)(2,1)S(1)}, bf16[272,512]{1,0:T(8,128)(2,1)S(1)}, u32[]{:S(2)}, u32[]{:S(2)}) collective-permute-start(bf16[272,512]{1,0:T(8,128)(2,1)S(1)} %broadcast_select_fusion), channel_id=1, source_target_pairs={{0,8},{104,64},{16,24},{120,80},{32,40},{8,96},{48,56},{24,112},{6... | collective-permute-start | bytes 835592 | tf_op jit(solution)/shard_map/ppermute | solution.py:434
  37.1 6.2 %collective-permute-start.6 = (bf16[272,512]{1,0:T(8,128)(2,1)S(1)}, bf16[272,512]{1,0:T(8,128)(2,1)S(1)}, u32[]{:S(2)}, u32[]{:S(2)}) collective-permute-start(bf16[272,512]{1,0:T(8,128)(2,1)S(1)} %collective-permute-done.5.refs_6_), channel_id=1, source_target_pairs={{0,8},{8,0},{16,24},{24,16},{32,40},{40,32},{48,56},{56,48},{64,72... | collective-permute-start | bytes 835592 | tf_op jit(solution)/shard_map/ppermute | solution.py:400

commit v4 on v3

--- a/solution.py
+++ b/solution.py
@@ -333,11 +333,11 @@
         known = jnp.where(lane_row == 16 + g, x[4:5, 0:1], known)
         known = jnp.where(lane_row == 24 + g, x[5:6, 0:1], known)
     table = jnp.concatenate(fields, axis=1)
-    table = jnp.concatenate([table, jnp.zeros((HD - 16, 8 * HD), F32)], axis=0)
     onehot = jnp.concatenate(onehots, axis=1)
     moved = 0.0
     for part in three(table):
         moved = moved + lax.dot_general(onehot, part, NT, preferred_element_type=F32)
+    moved = jnp.concatenate([moved, jnp.zeros((64, HD - 16), F32)], axis=1)
     out_ref[...] = moved + known
 
 

time: 101 us -> 98.6 us (0.976); the launches traced: 99.9 us -> 98.8 us
  Pallas kernels: 15.5 us -> 12.6 us
  blocking collectives: 46.8 us -> 48.7 us
    all_to_all x1, blocking collectives: 15.3 us -> 19.8 us  [shards(): lax.all_to_all(payload, 'group', split_axis=0, concat_axis=0, tiled=True)]
    pallas_call x2, Pallas kernels: 9.89 us -> 6.9 us  [attend(): pl.pallas_call(lambda *refs: attend_kernel(slots, len(msgs), len(befores)...]
    all_to_all x1, blocking collectives: 31.5 us -> 28.9 us  [shards(): lax.all_to_all(arranged, 'seq', split_axis=0, concat_axis=0, tiled=True)]
where the time goes in v4:
time: 98.6 us; the launch traced here: 98.8 us
  blocking collectives  48.7 us (49%)
  starting transfers between devices  28.2 us (29%)
  Pallas kernels  12.6 us (13%)
  waiting for transfers between devices  5.12 us (5%)
  local copies, waits for them, and re-layouts  3.25 us (3%)
    all_to_all x1, blocking collectives, shards(): lax.all_to_all(arranged, 'seq', split_axis=0, concat_axis=0, tiled=True)  28.9 us
    all_to_all x1, blocking collectives, shards(): lax.all_to_all(payload, 'group', split_axis=0, concat_axis=0, tiled=True)  19.8 us
    ppermute x3, starting transfers between devices, hop(): lax.ppermute(value, 'seq', [(s, s + 2 * chips) for s in range(count - 2 *...  13.5 us
    pallas_call x2, Pallas kernels, attend(): pl.pallas_call(lambda *refs: attend_kernel(slots, len(msgs), len(befores)...  6.9 us
    ppermute x1, starting transfers between devices, shards(): far = lax.ppermute(sent, 'seq', last)  5.15 us
    ppermute x1, starting transfers between devices, shards(): relayed = lax.ppermute(own, 'seq', back)  4.97 us
    ppermute x2, starting transfers between devices, swap(): return lax.ppermute(value, 'seq', [(s, s ^ 1) for s in range(count)])  4.59 us
    ppermute x1, waiting for transfers between devices, shards(): far = lax.ppermute(sent, 'seq', last)  4.24 us
  transfers between devices with their start and end apart: 7, of which 2 were waited for; matrix products, arithmetic and copies ran while one was open for 0% of the time, Pallas kernels for 4%

profile of v4, /device:TPU:1, one launch (start us, length us, event | category | flops | bytes accessed | tf_op | source)
XLA Modules:
  0.0 98.8 jit_solution(13829745477877677199)
XLA Ops:
  0.6 1.9 %message.1.refs_3_ = bf16[272,512]{1,0:T(8,128)(2,1)} custom-call(bf16[256,1024]{1,0:T(8,128)(2,1)} %bitcast.15, bf16[32,128]{1,0:T(8,128)(2,1)} %bitcast.18), custom_call_target="tpu_custom_call" | custom-call | flops 8388608 | bytes 800000 | tf_op jit(solution)/shard_map/message/pallas_call | solution.py:62
  2.6 4.0 %collective-permute-start = (bf16[272,512]{1,0:T(8,128)(2,1)}, bf16[272,512]{1,0:T(8,128)(2,1)S(1)}, u32[]{:S(2)}, u32[]{:S(2)}) collective-permute-start(bf16[272,512]{1,0:T(8,128)(2,1)} %message.1.refs_3_), channel_id=1, source_target_pairs={{0,16},{8,24},{16,32},{24,40},{32,48},{40,56},{48,64},{56,72},{64,... | collective-permute-start | bytes 835592 | tf_op jit(solution)/shard_map/ppermute | solution.py:404
  6.6 5.0 %collective-permute-start.2 = (bf16[272,512]{1,0:T(8,128)(2,1)}, bf16[272,512]{1,0:T(8,128)(2,1)S(1)}, u32[]{:S(2)}, u32[]{:S(2)}) collective-permute-start(bf16[272,512]{1,0:T(8,128)(2,1)} %message.1.refs_3_), channel_id=1, source_target_pairs={{8,104},{24,120},{40,8},{56,24},{72,40},{88,56},{104,72},{120,88},... | collective-permute-start | bytes 835592 | tf_op jit(solution)/shard_map/ppermute | solution.py:429
  11.6 1.3 %collective-permute-start.1 = (bf16[272,512]{1,0:T(8,128)(2,1)}, bf16[272,512]{1,0:T(8,128)(2,1)S(1)}, u32[]{:S(2)}, u32[]{:S(2)}) collective-permute-start(bf16[272,512]{1,0:T(8,128)(2,1)} %message.1.refs_3_), channel_id=1, source_target_pairs={{0,32},{8,40},{16,48},{24,56},{32,64},{40,72},{48,80},{56,88},{64,... | collective-permute-start | bytes 835592 | tf_op jit(solution)/shard_map/ppermute | solution.py:404
  12.9 0.0 collective-permute-done.refs_4_
  12.9 0.0 copy-start
  12.9 1.6 %copy-done = bf16[1,256,4096]{2,1,0:T(8,128)(2,1)S(1)} copy-done((bf16[1,256,4096]{2,1,0:T(8,128)(2,1)S(1)}, bf16[1,256,4096]{2,1,0:T(8,128)(2,1)}, u32[]{:S(2)}) %copy-start) | copy-done | bytes 2097176
  14.5 1.0 copy-done.2
  15.5 0.7 copy-done.3
  16.2 3.9 %attend.2.refs_8_ = f32[2,256,128]{2,1,0:T(8,128)S(1)} custom-call(s32[1]{0:T(128)} %bitcast.refs_0_, s32[2,8]{1,0:T(2,128)S(1)} %bitcast.13, bf16[256,4096]{1,0:T(8,128)(2,1)S(1)} %bitcast.11, bf16[272,512]{1,0:T(8,128)(2,1)S(1)} %copy-done.2, bf16[272,512]{1,0:T(8,128)(2,1)S(1)} %collective-permute-done.refs_4_), custom_call_target="tpu_custom_call" | custom-call | flops 1000000 | bytes 100000 | tf_op jit(solution)/shard_map/attend/pallas_call | solution.py:293
  20.1 0.0 copy-start.4
  20.1 0.0 copy-start.5
  20.1 0.0 copy-start.6
  20.1 0.0 copy-start.7
  20.1 0.0 collective-permute-done.2
  20.2 0.9 collective-permute-done.1.refs_4_
  21.1 8.2 %collective-permute-start.5 = (bf16[272,512]{1,0:T(8,128)(2,1)S(1)}, bf16[272,512]{1,0:T(8,128)(2,1)S(1)}, u32[]{:S(2)}, u32[]{:S(2)}) collective-permute-start(bf16[272,512]{1,0:T(8,128)(2,1)S(1)} %collective-permute-done.1.refs_4_), channel_id=1, source_target_pairs={{0,16},{8,24},{16,32},{24,40},{32,48},{40,56},{48,64},{56,72},{64,... | collective-permute-start | bytes 835592 | tf_op jit(solution)/shard_map/ppermute | solution.py:404
  29.3 2.7 %collective-permute-start.3 = (bf16[544,512]{1,0:T(8,128)(2,1)S(1)}, bf16[544,512]{1,0:T(8,128)(2,1)S(1)}, u32[]{:S(2)}, u32[]{:S(2)}) collective-permute-start(bf16[544,512]{1,0:T(8,128)(2,1)S(1)} %pad_maximum_fusion), channel_id=1, source_target_pairs={{0,8},{8,0},{16,24},{24,16},{32,40},{40,32},{48,56},{56,48},{64,72... | collective-permute-start | bytes 1671176 | tf_op jit(solution)/shard_map/ppermute | solution.py:400
  32.0 5.1 %collective-permute-start.4 = (bf16[272,512]{1,0:T(8,128)(2,1)S(1)}, bf16[272,512]{1,0:T(8,128)(2,1)S(1)}, u32[]{:S(2)}, u32[]{:S(2)}) collective-permute-start(bf16[272,512]{1,0:T(8,128)(2,1)S(1)} %broadcast_select_fusion), channel_id=1, source_target_pairs={{0,8},{104,64},{16,24},{120,80},{32,40},{8,96},{48,56},{24,112},{6... | collective-permute-start | bytes 835592 | tf_op jit(solution)/shard_map/ppermute | solution.py:434
  37.1 0.0 collective-permute-done.5.refs_6_
  37.1 1.9 %collective-permute-start.6 = (bf16[272,512]{1,0:T(8,128)(2,1)S(1)}, bf16[272,512]{1,0:T(8,128)(2,1)S(1)}, u32[]{:S(2)}, u32[]{:S(2)}) collective-permute-start(bf16[272,512]{1,0:T(8,128)(2,1)S(1)} %collective-permute-done.5.refs_6_), channel_id=1, source_target_pairs={{0,8},{8,0},{16,24},{24,16},{32,40},{40,32},{48,56},{56,48},{64,72... | collective-permute-start | bytes 835592 | tf_op jit(solution)/shard_map/ppermute | solution.py:400
  39.1 4.2 %collective-permute-done.4.refs_5_ = bf16[272,512]{1,0:T(8,128)(2,1)S(1)} collective-permute-done((bf16[272,512]{1,0:T(8,128)(2,1)S(1)}, bf16[272,512]{1,0:T(8,128)(2,1)S(1)}, u32[]{:S(2)}, u32[]{:S(2)}) %collective-permute-start.4) | collective-permute-done | bytes 278560 | tf_op jit(solution)/shard_map/ppermute | solution.py:434
  43.3 0.0 collective-permute-done.3.refs_3_
  43.3 0.0 collective-permute-done.6.refs_7_
  43.3 0.0 copy-done.1
  43.3 0.0 copy-done.4
  43.3 0.0 copy-done.5
  43.4 3.0 %attend.3 = (f32[1,256]{1,0:T(1,128)}, f32[8,8,128]{2,1,0:T(8,128)S(1)}) custom-call(s32[1]{0:T(128)} %bitcast.refs_0_, s32[2,8]{1,0:T(2,128)S(1)} %bitcast.14, bf16[256,4096]{1,0:T(8,128)(2,1)S(1)} %bitcast.12, bf16[544,512]{1,0:T(8,128)(2,1)S(1)} %collective-permute-done.3.refs_3_, bf16[272,512]{1,0:T(8,128)(2,1)S(1)} %collective-permute-done.1.refs_4_, ...), custom_call_target="tpu_custom_call" | custom-call | flops 1000000 | bytes 100000 | tf_op jit(solution)/shard_map/attend/pallas_call | solution.py:293
  46.3 19.8 %all_to_all.16.in_ref = f32[8,8,128]{2,1,0:T(8,128)} all-to-all(f32[8,8,128]{2,1,0:T(8,128)S(1)} %get-tuple-element.16), channel_id=1, replica_groups=mesh['seq'=64,'group'=8] {'group'}, dimensions={0} | all-to-all | bytes 65536 | tf_op jit(solution)/shard_map/all_to_all | solution.py:439
  66.1 1.9 %sort_part.1 = f32[64,128]{1,0:T(8,128)} custom-call(f32[8,8,128]{2,1,0:T(8,128)} %all_to_all.16.in_ref), custom_call_target="tpu_custom_call" | custom-call | flops 10000000 | bytes 70000 | tf_op jit(solution)/shard_map/sort_part/pallas_call | solution.py:345
  68.1 28.9 %all_to_all.17 = f32[64,1,128]{2,1,0:T(1,128)} all-to-all(f32[64,1,128]{2,1,0:T(1,128)} %bitcast.17), channel_id=1, replica_groups=mesh['seq'=64,'group'=8] {'seq'}, dimensions={0} | all-to-all | bytes 65536 | tf_op jit(solution)/shard_map/all_to_all | solution.py:441
  97.0 1.8 %finish.1 = (f32[1,256]{1,0:T(1,128)}, f32[1,256]{1,0:T(1,128)}) custom-call(f32[64,128]{1,0:T(8,128)} %bitcast.16), custom_call_target="tpu_custom_call" | custom-call | flops 500000 | bytes 40000 | tf_op jit(solution)/shard_map/finish/pallas_call | solution.py:386
  (7 shorter events, 0.1 us)
Async XLA Ops:
  2.6 10.4 %collective-permute-start = (bf16[272,512]{1,0:T(8,128)(2,1)}, bf16[272,512]{1,0:T(8,128)(2,1)S(1)}, u32[]{:S(2)}, u32[]{:S(2)}) collective-permute-start(bf16[272,512]{1,0:T(8,128)(2,1)} %message.1.refs_3_), channel_id=1, source_target_pairs={{0,16},{8,24},{16,32},{24,40},{32,48},{40,56},{48,64},{56,72},{64,... | collective-permute-start | bytes 835592 | tf_op jit(solution)/shard_map/ppermute | solution.py:404
  6.6 13.5 %collective-permute-start.2 = (bf16[272,512]{1,0:T(8,128)(2,1)}, bf16[272,512]{1,0:T(8,128)(2,1)S(1)}, u32[]{:S(2)}, u32[]{:S(2)}) collective-permute-start(bf16[272,512]{1,0:T(8,128)(2,1)} %message.1.refs_3_), channel_id=1, source_target_pairs={{8,104},{24,120},{40,8},{56,24},{72,40},{88,56},{104,72},{120,88},... | collective-permute-start | bytes 835592 | tf_op jit(solution)/shard_map/ppermute | solution.py:429
  11.6 9.5 %collective-permute-start.1 = (bf16[272,512]{1,0:T(8,128)(2,1)}, bf16[272,512]{1,0:T(8,128)(2,1)S(1)}, u32[]{:S(2)}, u32[]{:S(2)}) collective-permute-start(bf16[272,512]{1,0:T(8,128)(2,1)} %message.1.refs_3_), channel_id=1, source_target_pairs={{0,32},{8,40},{16,48},{24,56},{32,64},{40,72},{48,80},{56,88},{64,... | collective-permute-start | bytes 835592 | tf_op jit(solution)/shard_map/ppermute | solution.py:404
  12.9 1.6 %copy-start = (bf16[1,256,4096]{2,1,0:T(8,128)(2,1)S(1)}, bf16[1,256,4096]{2,1,0:T(8,128)(2,1)}, u32[]{:S(2)}) copy-start(bf16[1,256,4096]{2,1,0:T(8,128)(2,1)} %param.8) | copy-start | bytes 6291460
  14.5 1.0 copy-start.2
  15.5 0.7 copy-start.3
  16.1 27.2 %copy-start.1 = (bf16[1,256,4096]{2,1,0:T(8,128)(2,1)S(1)}, bf16[1,256,4096]{2,1,0:T(8,128)(2,1)}, u32[]{:S(2)}) copy-start(bf16[1,256,4096]{2,1,0:T(8,128)(2,1)} %param.8) | copy-start | bytes 6291460
  20.1 23.2 %copy-start.4 = (f32[1,256]{1,0:T(1,128)S(1)}, f32[1,256]{1,0:T(1,128)}, u32[]{:S(2)}) copy-start(f32[1,256]{1,0:T(1,128)} %refs_9_.1) | copy-start | bytes 3076
  20.1 23.2 %copy-start.5 = (s32[1,256]{1,0:T(1,128)S(1)}, s32[1,256]{1,0:T(1,128)}, u32[]{:S(2)}) copy-start(s32[1,256]{1,0:T(1,128)} %refs_10_.1) | copy-start | bytes 3076
  20.1 23.2 %copy-start.6 = (f32[1,256]{1,0:T(1,128)S(1)}, f32[1,256]{1,0:T(1,128)}, u32[]{:S(2)}) copy-start(f32[1,256]{1,0:T(1,128)} %refs_11_.1) | copy-start | bytes 3076
  20.1 23.2 %copy-start.7 = (s32[1,256]{1,0:T(1,128)S(1)}, s32[1,256]{1,0:T(1,128)}, u32[]{:S(2)}) copy-start(s32[1,256]{1,0:T(1,128)} %refs_12_.1) | copy-start | bytes 3076
  21.1 16.1 %collective-permute-start.5 = (bf16[272,512]{1,0:T(8,128)(2,1)S(1)}, bf16[272,512]{1,0:T(8,128)(2,1)S(1)}, u32[]{:S(2)}, u32[]{:S(2)}) collective-permute-start(bf16[272,512]{1,0:T(8,128)(2,1)S(1)} %collective-permute-done.1.refs_4_), channel_id=1, source_target_pairs={{0,16},{8,24},{16,32},{24,40},{32,48},{40,56},{48,64},{56,72},{64,... | collective-permute-start | bytes 835592 | tf_op jit(solution)/shard_map/ppermute | solution.py:404
  29.3 14.0 %collective-permute-start.3 = (bf16[544,512]{1,0:T(8,128)(2,1)S(1)}, bf16[544,512]{1,0:T(8,128)(2,1)S(1)}, u32[]{:S(2)}, u32[]{:S(2)}) collective-permute-start(bf16[544,512]{1,0:T(8,128)(2,1)S(1)} %pad_maximum_fusion), channel_id=1, source_target_pairs={{0,8},{8,0},{16,24},{24,16},{32,40},{40,32},{48,56},{56,48},{64,72... | collective-permute-start | bytes 1671176 | tf_op jit(solution)/shard_map/ppermute | solution.py:400
  32.0 11.3 %collective-permute-start.4 = (bf16[272,512]{1,0:T(8,128)(2,1)S(1)}, bf16[272,512]{1,0:T(8,128)(2,1)S(1)}, u32[]{:S(2)}, u32[]{:S(2)}) collective-permute-start(bf16[272,512]{1,0:T(8,128)(2,1)S(1)} %broadcast_select_fusion), channel_id=1, source_target_pairs={{0,8},{104,64},{16,24},{120,80},{32,40},{8,96},{48,56},{24,112},{6... | collective-permute-start | bytes 835592 | tf_op jit(solution)/shard_map/ppermute | solution.py:434
  37.1 6.2 %collective-permute-start.6 = (bf16[272,512]{1,0:T(8,128)(2,1)S(1)}, bf16[272,512]{1,0:T(8,128)(2,1)S(1)}, u32[]{:S(2)}, u32[]{:S(2)}) collective-permute-start(bf16[272,512]{1,0:T(8,128)(2,1)S(1)} %collective-permute-done.5.refs_6_), channel_id=1, source_target_pairs={{0,8},{8,0},{16,24},{24,16},{32,40},{40,32},{48,56},{56,48},{64,72... | collective-permute-start | bytes 835592 | tf_op jit(solution)/shard_map/ppermute | solution.py:400
